TPU v7x, 32 devices: a whole 2x2x4 slice. The times are simulated.
32 devices in a mesh: dp: 16 (over z, x, core), tensor: 2 (over y).
Axes of the slice: x: 2, y: 2, z: 4, core: 2. Of those that a mesh axis runs over, the one named last changes fastest.
Arguments:
- latent_tokens: float32 [16384, 1152], P(('dp', 'tensor')), may hold values from -6 to 6
- conditioning: float32 [16, 1152], P('dp'), may hold values from -6 to 6
- out_grad: float32 [16384, 1152], P(('dp', 'tensor')), may hold values from -6 to 6
- qkv_weight: float32 [1152, 3, 1152], P('dp', None, 'tensor'), may hold values from -0.1875 to 0.1875
- qkv_bias: float32 [2, 1152], P(None, 'tensor'), may hold values from -1.25 to 1.25
- proj_weight: float32 [1152, 1152], P('tensor', 'dp'), may hold values from -0.75 to 0.75
- proj_bias: float32 [1152], replicated, may hold values from -1.75 to 1.75
- first_layer_weight: float32 [1152, 4608], P('dp', 'tensor'), may hold values from -0.1875 to 0.1875
- fc1_bias: float32 [4608], P('tensor'), may hold values from -3 to 3
- fc2_weight: float32 [4608, 1152], P('tensor', 'dp'), may hold values from -0.09375 to 0.09375
- second_layer_bias: float32 [1152], replicated, may hold values from -1.75 to 1.75
- ada_weight: float32 [1152, 6, 1152], P('dp', None, 'tensor'), may hold values from -0.1875 to 0.1875
- ada_bias: float32 [6, 1152], P(None, 'tensor'), may hold values from -3 to 3
Outputs:
- layer_out: float32 [16384, 1152], P(('dp', 'tensor'))
- tokens_grad: float32 [16384, 1152], P(('dp', 'tensor'))
- conditioning_grad: float32 [16, 1152], P('dp')
- qkv_weight_grad: float32 [1152, 3, 1152], P('dp', None, 'tensor')
- qkv_bias_grad: float32 [2, 1152], P(None, 'tensor')
- proj_weight_grad: float32 [1152, 1152], P('tensor', 'dp')
- proj_bias_grad: float32 [1152], replicated
- fc1_weight_grad: float32 [1152, 4608], P('dp', 'tensor')
- first_layer_bias_gradient: float32 [4608], P('tensor')
- fc2_weight_grad: float32 [4608, 1152], P('tensor', 'dp')
- fc2_bias_grad: float32 [1152], replicated
- ada_weight_grad: float32 [1152, 6, 1152], P('dp', None, 'tensor')
- ada_bias_grad: float32 [6, 1152], P(None, 'tensor')
All inputs are finite; a program needn't handle non-finite values.
Results may differ from a plain program's by a relative error of at most 0.012.
The roundings to bfloat16 on the way count: a program that leaves them out, or rounds other values in their place, can miss the bound.
Values may be sent and summed in bfloat16 or wider, within the bound.
A program may use at most 256 MiB of HBM per device.

v0:
```python
import jax
import jax.numpy as jnp
from jax import lax
from jax.sharding import PartitionSpec as P

HEAD_DIM = 72
SEQ = 1024


highest_precision_mode = lax.Precision.HIGHEST
epsilon = 1e-06


def gelu_tanh(values):
    return jax.nn.gelu(values, approximate=True)


def normalize(values):
    center = values - jnp.mean(values, axis=-1, keepdims=True)
    scaled = lax.rsqrt(jnp.mean(center * center, axis=-1, keepdims=True) + epsilon)
    return (center * scaled, scaled)


def norm_back(grad, normed, scaled):
    first = jnp.mean(grad, axis=-1, keepdims=True)
    second = jnp.mean(grad * normed, axis=-1, keepdims=True)
    return (grad - first - normed * second) * scaled


def body(
    latent_tokens,
    conditioning,
    out_grad,
    qkv_weight,
    qkv_bias,
    proj_weight,
    proj_bias,
    first_layer_weight,
    fc1_bias,
    fc2_weight,
    second_layer_bias,
    ada_weight,
    ada_bias,
):

    def fetch():
        return (
            lax.all_gather(qkv_weight.astype(jnp.bfloat16), "dp", axis=0, tiled=True),
            lax.all_gather(proj_weight.astype(jnp.bfloat16), "dp", axis=1, tiled=True),
            lax.all_gather(first_layer_weight.astype(jnp.bfloat16), "dp", axis=0, tiled=True),
            lax.all_gather(fc2_weight.astype(jnp.bfloat16), "dp", axis=1, tiled=True),
            lax.all_gather(ada_weight.astype(jnp.bfloat16), "dp", axis=0, tiled=True),
        )

    w_qkv, w_proj, w_fc1, w_fc2, w_ada = fetch()
    tok_rows, width_full = latent_tokens.shape
    latents = conditioning.shape[0]
    group_rows = tok_rows * lax.axis_size("tensor")
    width = w_qkv.shape[2]
    heads_local = width // HEAD_DIM
    factor = HEAD_DIM ** (-0.5)
    silu_cond, silu_pull = jax.vjp(jax.nn.silu, conditioning)
    cond_low = silu_cond.astype(jnp.bfloat16)
    mod_part = (
        jnp.einsum("ld,dkf->lkf", cond_low, w_ada, preferred_element_type=jnp.float32) + ada_bias
    )
    modulation_values = lax.all_gather(mod_part, "tensor", axis=2, tiled=True)
    span = min(tok_rows, SEQ)
    block_count = tok_rows // span
    first_row = lax.axis_index("tensor") * tok_rows
    block_latent = (first_row + jnp.arange(block_count, dtype=jnp.int32) * span) // SEQ
    select_helper = (block_latent[:, None] == jnp.arange(latents, dtype=jnp.int32)[None, :]).astype(
        jnp.float32
    )
    block_modulation_terms = jnp.einsum(
        "pe,egt->pgt", select_helper, modulation_values, precision=highest_precision_mode
    )

    def spread(values):
        return jnp.broadcast_to(values[:, None, :], (block_count, span, width_full)).reshape(
            tok_rows, width_full
        )

    def per_latent(values):
        sums = jnp.sum(values.reshape(block_count, span, width_full), axis=1)
        return jnp.einsum("bl,bd->ld", select_helper, sums, precision=highest_precision_mode)

    shift_one = spread(block_modulation_terms[:, 0])
    scale_one = spread(block_modulation_terms[:, 1])
    gate_one = spread(block_modulation_terms[:, 2])
    shift_two = spread(block_modulation_terms[:, 3])
    scale_two = spread(block_modulation_terms[:, 4])
    gate_two = spread(block_modulation_terms[:, 5])
    normed_one, rscale_one = normalize(latent_tokens)
    attn_input = (normed_one * (1.0 + scale_one) + shift_one).astype(jnp.bfloat16)
    qkv_shift = jnp.stack([qkv_bias[0], jnp.zeros_like(qkv_bias[0]), qkv_bias[1]])
    piece = lax.all_gather(attn_input, "tensor", axis=0, tiled=True)
    rows_buf = piece
    made = jnp.einsum("rd,dkf->rkf", piece, w_qkv, preferred_element_type=jnp.float32) + qkv_shift
    made_buf = made.astype(jnp.bfloat16)
    attn_rows = rows_buf
    qkv_all = made_buf
    qkv_latent = qkv_all.reshape(group_rows // SEQ, SEQ, 3, heads_local, HEAD_DIM)

    def attend(block):
        query, keys, values = (block[:, 0], block[:, 1], block[:, 2])
        scores = (
            jnp.einsum("qhd,khd->hqk", query, keys, preferred_element_type=jnp.float32) * factor
        )
        peak = jnp.max(scores, axis=-1, keepdims=True)
        expo = jnp.exp(scores - peak)
        total = jnp.sum(expo, axis=-1, keepdims=True)
        probs = (expo / total).astype(jnp.bfloat16)
        result = jnp.einsum("hqk,khd->qhd", probs, values, preferred_element_type=jnp.float32)
        return (result.astype(jnp.bfloat16), peak[..., 0] + jnp.log(total[..., 0]))

    attn_low, logsum = lax.map(attend, qkv_latent)
    attn_low = attn_low.reshape(group_rows, width)
    rows = attn_low
    branch_one = (
        lax.psum_scatter(
            jnp.dot(rows, w_proj, preferred_element_type=jnp.float32),
            "tensor",
            scatter_dimension=0,
            tiled=True,
        )
        + proj_bias
    )
    middle = latent_tokens + gate_one * branch_one
    normed_two, rscale_two = normalize(middle)
    mlp_input = (normed_two * (1.0 + scale_two) + shift_two).astype(jnp.bfloat16)
    piece = lax.all_gather(mlp_input, "tensor", axis=0, tiled=True)
    rows_buf = piece
    made = jnp.dot(piece, w_fc1, preferred_element_type=jnp.float32) + fc1_bias
    made_buf = made
    act, gelu_pull = jax.vjp(gelu_tanh, made_buf)
    act_low = act.astype(jnp.bfloat16)
    rows = act_low
    branch_two = (
        lax.psum_scatter(
            jnp.dot(rows, w_fc2, preferred_element_type=jnp.float32).astype(jnp.bfloat16),
            "tensor",
            scatter_dimension=0,
            tiled=True,
        ).astype(jnp.float32)
        + second_layer_bias
    )
    layer_out = middle + gate_two * branch_two
    w_qkv, w_proj, w_fc1, w_fc2, w_ada = fetch()
    d_gate_two = per_latent(out_grad * branch_two)
    grad_m = (gate_two * out_grad).astype(jnp.bfloat16)
    fc2_bias_part = jnp.sum(grad_m.astype(jnp.float32), axis=0)
    piece = lax.all_gather(grad_m, "tensor", axis=0, tiled=True)
    made = jnp.einsum("rd,fd->rf", piece, w_fc2, preferred_element_type=jnp.float32)
    act_buf = made
    weight_acc = jnp.einsum("rf,rd->fd", act_low, piece, preferred_element_type=jnp.float32)
    grad_fc2 = weight_acc
    grad_pre = gelu_pull(act_buf)[0].astype(jnp.bfloat16)
    fc1_bias_part = jnp.sum(grad_pre.astype(jnp.float32), axis=0)
    grad_fc1 = jnp.einsum("rd,rf->df", rows_buf, grad_pre, preferred_element_type=jnp.float32)
    rows = grad_pre
    grad_h_two = lax.psum_scatter(
        jnp.einsum("rf,df->rd", rows, w_fc1, preferred_element_type=jnp.float32),
        "tensor",
        scatter_dimension=0,
        tiled=True,
    )
    d_shift_two = per_latent(grad_h_two)
    d_scale_two = per_latent(grad_h_two * normed_two)
    grad_mid = out_grad + norm_back(grad_h_two * (1.0 + scale_two), normed_two, rscale_two)
    d_gate_one = per_latent(grad_mid * branch_one)
    grad_z = (gate_one * grad_mid).astype(jnp.bfloat16)
    proj_bias_part = jnp.sum(grad_z.astype(jnp.float32), axis=0)
    piece = lax.all_gather(grad_z, "tensor", axis=0, tiled=True)
    made = jnp.einsum("rd,fd->rf", piece, w_proj, preferred_element_type=jnp.float32)
    weight_acc = jnp.einsum("rf,rd->fd", attn_low, piece, preferred_element_type=jnp.float32)
    grad_attn_low = made.astype(jnp.bfloat16).reshape(group_rows // SEQ, SEQ, heads_local, HEAD_DIM)

    def attend_back(block):
        packed, grad_o, lse = block
        query, keys, values = (packed[:, 0], packed[:, 1], packed[:, 2])
        scores = (
            jnp.einsum("qhd,khd->hqk", query, keys, preferred_element_type=jnp.float32) * factor
        )
        probs = jnp.exp(scores - lse[..., None])
        probs_low = probs.astype(jnp.bfloat16)
        grad_p = jnp.einsum("qhd,khd->hqk", grad_o, values, preferred_element_type=jnp.float32)
        grad_v = jnp.einsum("hqk,qhd->khd", probs_low, grad_o, preferred_element_type=jnp.float32)
        delta = jnp.sum(grad_p * probs, axis=-1, keepdims=True)
        grad_s = (probs * (grad_p - delta)).astype(jnp.bfloat16)
        grad_q = (
            jnp.einsum("hqk,khd->qhd", grad_s, keys, preferred_element_type=jnp.float32) * factor
        )
        grad_k = (
            jnp.einsum("hqk,qhd->khd", grad_s, query, preferred_element_type=jnp.float32) * factor
        )
        return jnp.stack([grad_q, grad_k, grad_v], axis=1).astype(jnp.bfloat16)

    grad_qkv = lax.map(attend_back, (qkv_latent, grad_attn_low, logsum)).reshape(
        group_rows, 3, width
    )
    qkv_bias_part = jnp.sum(grad_qkv.astype(jnp.float32), axis=0)
    grad_qkv_weight = jnp.einsum(
        "rd,rkf->dkf", attn_rows, grad_qkv, preferred_element_type=jnp.float32
    )
    rows = grad_qkv
    grad_h_one = lax.psum_scatter(
        jnp.einsum("rkf,dkf->rd", rows, w_qkv, preferred_element_type=jnp.float32),
        "tensor",
        scatter_dimension=0,
        tiled=True,
    )
    d_shift_one = per_latent(grad_h_one)
    d_scale_one = per_latent(grad_h_one * normed_one)
    tokens_grad = grad_mid + norm_back(grad_h_one * (1.0 + scale_one), normed_one, rscale_one)
    grad_mods = jnp.stack(
        [d_shift_one, d_scale_one, d_gate_one, d_shift_two, d_scale_two, d_gate_two], axis=1
    )
    mods_share = lax.psum_scatter(grad_mods, "tensor", scatter_dimension=2, tiled=True)
    grad_ada = jnp.einsum(
        "ld,lkf->dkf", cond_low.astype(jnp.float32), mods_share, precision=highest_precision_mode
    )
    grad_ada_bias = jnp.sum(mods_share, axis=0)
    cond_part = jnp.einsum(
        "lkf,dkf->ld", mods_share, w_ada.astype(jnp.float32), precision=highest_precision_mode
    )
    tensor_totals = lax.psum((cond_part, proj_bias_part, fc2_bias_part), "tensor")
    conditioning_grad = silu_pull(tensor_totals[0])[0]
    weight_totals = (
        lax.psum_scatter(grad_qkv_weight, "dp", scatter_dimension=0, tiled=True),
        lax.psum_scatter(weight_acc, "dp", scatter_dimension=1, tiled=True),
        lax.psum_scatter(grad_fc1, "dp", scatter_dimension=0, tiled=True),
        lax.psum_scatter(grad_fc2, "dp", scatter_dimension=1, tiled=True),
        lax.psum_scatter(grad_ada, "dp", scatter_dimension=0, tiled=True),
    )
    qkv_bias_pair = jnp.stack([qkv_bias_part[0], qkv_bias_part[2]])
    bias_totals = lax.psum(
        (qkv_bias_pair, tensor_totals[1], fc1_bias_part, tensor_totals[2], grad_ada_bias), "dp"
    )
    return (
        layer_out,
        tokens_grad,
        conditioning_grad,
        weight_totals[0],
        bias_totals[0],
        weight_totals[1],
        bias_totals[1],
        weight_totals[2],
        bias_totals[2],
        weight_totals[3],
        bias_totals[3],
        weight_totals[4],
        bias_totals[4],
    )


def solution(mesh):
    in_specs = (
        P(("dp", "tensor"), None),
        P("dp", None),
        P(("dp", "tensor"), None),
        P("dp", None, "tensor"),
        P(None, "tensor"),
        P("tensor", "dp"),
        P(),
        P("dp", "tensor"),
        P("tensor"),
        P("tensor", "dp"),
        P(),
        P("dp", None, "tensor"),
        P(None, "tensor"),
    )
    out_specs = (
        P(("dp", "tensor"), None),
        P(("dp", "tensor"), None),
        P("dp", None),
        P("dp", None, "tensor"),
        P(None, "tensor"),
        P("tensor", "dp"),
        P(),
        P("dp", "tensor"),
        P("tensor"),
        P("tensor", "dp"),
        P(),
        P("dp", None, "tensor"),
        P(None, "tensor"),
    )
    return jax.shard_map(body, mesh=mesh, in_specs=in_specs, out_specs=out_specs, check_vma=False)
```

profile of v0, /device:TPU:0, one launch (start us, length us, event | category | flops | bytes accessed | tf_op | source)
XLA Modules:
  0.0 1487.2 jit_solution(656812246788620732)
XLA Ops:
  7.2 2.3 convert_element_type.91
  11.8 79.5 %all-gather.12.cloned.1.call-done = bf16[1152,6,576]{2,0,1:T(8,128)(2,1)} async-done(((bf16[72,6,576]{2,0,1:T(8,128)(2,1)}), bf16[1152,6,576]{2,0,1:T(8,128)(2,1)}) %all-gather.12.cloned.1.call-update) | async-done | bytes 7962640 | tf_op jit(solution)/shard_map/all_gather | solution.py:52
  91.3 4.8 fusion.27
  96.1 4.5 all-gather.1
  103.8 40.2 %all-gather.16.cloned.1.call-done = bf16[1152,3,576]{2,0,1:T(8,128)(2,1)} async-done(((bf16[72,3,576]{2,0,1:T(8,128)(2,1)}), bf16[1152,3,576]{2,0,1:T(8,128)(2,1)}) %all-gather.16.cloned.1.call-update) | async-done | bytes 3981328 | tf_op jit(solution)/shard_map/all_gather | solution.py:48
  144.0 36.7 %all-gather.14.cloned.1.call-done = bf16[1024,1152]{1,0:T(8,128)(2,1)} async-done(((bf16[512,1152]{1,0:T(8,128)(2,1)}), bf16[1024,1152]{1,0:T(8,128)(2,1)}) %all-gather.14.cloned.1.call-update) | async-done | bytes 2359312 | tf_op jit(solution)/shard_map/all_gather | solution.py:97
  180.8 7.8 add_convert_fusion
  188.5 13.4 multiply_reduce_fusion.1
  201.9 13.7 fusion
  215.7 14.4 fusion.18
  230.1 6.1 fusion.38
  238.1 58.3 %reduce-scatter.15.cloned.1.call-done = f32[512,1152]{1,0:T(8,128)} async-done(((f32[1024,1152]{1,0:T(8,128)}), f32[512,1152]{1,0:T(8,128)}) %reduce-scatter.15.cloned.1.call-update) | async-done | bytes 2359312 | tf_op jit(solution)/shard_map/reduce_scatter | solution.py:121
  302.3 53.3 %all-gather.22.cloned.1.call-done = bf16[1152,2304]{1,0:T(8,128)(2,1)} async-done(((bf16[72,2304]{1,0:T(8,128)(2,1)}), bf16[1152,2304]{1,0:T(8,128)(2,1)}) %all-gather.22.cloned.1.call-update) | async-done | bytes 5308432 | tf_op jit(solution)/shard_map/all_gather | solution.py:50
  355.6 36.9 %all-gather.20.cloned.1.call-done = bf16[1024,1152]{1,0:T(8,128)(2,1)} async-done(((bf16[512,1152]{1,0:T(8,128)(2,1)}), bf16[1024,1152]{1,0:T(8,128)(2,1)}) %all-gather.20.cloned.1.call-update) | async-done | bytes 2359312 | tf_op jit(solution)/shard_map/all_gather | solution.py:132
  392.4 11.7 fusion.39
  404.2 47.6 %all-gather.24.cloned.1.call-done = bf16[2304,1152]{0,1:T(8,128)(2,1)} async-done(((bf16[2304,72]{0,1:T(8,128)(2,1)}), bf16[2304,1152]{0,1:T(8,128)(2,1)}) %all-gather.24.cloned.1.call-update) | async-done | bytes 5308432 | tf_op jit(solution)/shard_map/all_gather | solution.py:51
  451.8 13.4 convolution_convert_fusion
  465.3 33.4 %reduce-scatter.17.cloned.1.call-done = bf16[512,1152]{1,0:T(8,128)(2,1)} async-done(((bf16[1024,1152]{1,0:T(8,128)(2,1)}), bf16[512,1152]{1,0:T(8,128)(2,1)}) %reduce-scatter.17.cloned.1.call-update) | async-done | bytes 1179664 | tf_op jit(solution)/shard_map/reduce_scatter | solution.py:140
  498.7 3.4 convert_reduce_fusion.2
  502.2 36.2 %all-gather.26.cloned.1.call-done = bf16[1024,1152]{1,0:T(8,128)(2,1)} async-done(((bf16[512,1152]{1,0:T(8,128)(2,1)}), bf16[1024,1152]{1,0:T(8,128)(2,1)}) %all-gather.26.cloned.1.call-update) | async-done | bytes 2359312 | tf_op jit(solution)/shard_map/all_gather | solution.py:153
  538.4 15.8 %convert_reduce_fusion = (f32[2304]{0:T(1024)}, bf16[1024,2304]{1,0:T(8,128)(2,1)S(1)}) fusion(f32[1024,2304]{1,0:T(8,128)} %fusion.39, f32[2304]{0:T(1024)S(1)} %copy-done.58, bf16[1024,1152]{1,0:T(8,128)(2,1)} %all-gather.26.cloned.1.call-done, bf16[2304,1152]{0,1:T(8,128)(2,1)} %all-gather.24.cloned.1.call-done), kind=kOutput, calls=%fused_computation.19 | convolution fusion | flops 5490079744 | bytes 21841920 | tf_op jit(solution)/shard_map/rd,fd->rf/dot_general | solution.py:154
  556.3 10.4 fusion.40
  566.8 60.1 %reduce-scatter.19.cloned.1.call-done = f32[512,1152]{1,0:T(8,128)} async-done(((f32[1024,1152]{1,0:T(8,128)}), f32[512,1152]{1,0:T(8,128)}) %reduce-scatter.19.cloned.1.call-update) | async-done | bytes 2359312 | tf_op jit(solution)/shard_map/reduce_scatter | solution.py:162
  626.9 3.4 multiply_reduce_fusion.3
  630.4 4.1 convert_reduce_fusion.3
  636.0 34.8 %all-gather.28.cloned.1.call-done = bf16[1024,1152]{1,0:T(8,128)(2,1)} async-done(((bf16[512,1152]{1,0:T(8,128)(2,1)}), bf16[1024,1152]{1,0:T(8,128)(2,1)}) %all-gather.28.cloned.1.call-update) | async-done | bytes 2359312 | tf_op jit(solution)/shard_map/all_gather | solution.py:174
  670.7 4.8 convolution_convert_fusion.1
  675.6 15.3 %fusion.15 = bf16[8,72,1024]{2,1,0:T(8,128)(2,1)} fusion(bf16[1024,8,72]{0,2,1:T(8,128)(2,1)} %bitcast.108, f32[8,1024,1024]{1,2,0:T(8,128)} %get-tuple-element.82, f32[8,1024]{1,0:T(8,128)} %log_add_fusion), kind=kOutput, calls=%fused_computation.56 | convolution fusion | flops 1233715200 | bytes 35946496 | tf_op jit(solution)/shard_map/while/body/eval_jaxpr/hqk,qhd->khd/dot_general | solution.py:188
  690.8 23.7 %multiply_reduce_fusion = (f32[8,1024]{1,0:T(8,128)}, f32[8,1024,1024]{1,2,0:T(8,128)}) fusion(f32[8,1024,1024]{1,2,0:T(8,128)} %get-tuple-element.82, f32[8,1024]{1,0:T(8,128)} %log_add_fusion, bf16[1024,8,72]{0,2,1:T(8,128)(2,1)} %bitcast.109, bf16[1024,3,8,72]{0,3,2,1:T(8,128)(2,1)S(1)} %bitcast.96), kind=kOutput, calls=%fused_computation.1 | convolution fusion | flops 1241505792 | bytes 69533696 | tf_op jit(solution)/shard_map/while/body/eval_jaxpr/qhd,khd->hqk/dot_general | solution.py:187
  714.5 28.4 %multiply_convert_fusion = bf16[8,1024,1024]{1,2,0:T(8,128)(2,1)} fusion(f32[8,1024,1024]{1,2,0:T(8,128)} %get-tuple-element.84, f32[8,1024,1024]{1,2,0:T(8,128)} %get-tuple-element.82, f32[8,1024]{1,0:T(8,128)} %get-tuple-element.83, f32[8,1024]{1,0:T(8,128)} %log_add_fusion), kind=kLoop, calls=%fused_computation | loop fusion | flops 41943040 | bytes 83951616 | tf_op jit(solution)/shard_map/while/body/eval_jaxpr/convert_element_type | solution.py:190
  743.0 12.0 multiply_convert_fusion.2
  755.0 8.9 multiply_convert_fusion.3
  764.9 9.9 convolution_bitcast_fusion
  775.6 59.4 %reduce-scatter.21.cloned.1.call-done = f32[512,1152]{1,0:T(8,128)} async-done(((f32[1024,1152]{1,0:T(8,128)}), f32[512,1152]{1,0:T(8,128)}) %reduce-scatter.21.cloned.1.call-update) | async-done | bytes 2359312 | tf_op jit(solution)/shard_map/reduce_scatter | solution.py:207
  835.1 2.8 multiply_reduce_fusion.5
  838.1 3.7 multiply_reduce_fusion.4
  843.2 5.7 fusion.41
  850.6 11.6 fusion.33
  863.8 10.5 fusion.42
  876.5 9.9 fusion.12
  888.8 8.1 broadcast_multiply_fusion
  897.7 9.4 convolution_bitcast_fusion.1
  907.1 7.3 all-reduce.2
  914.5 60.6 %all-reduce.1 = (f32[2,576]{1,0:T(2,128)}, f32[1152]{0:T(1024)}, f32[2304]{0:T(1024)}, f32[1152]{0:T(1024)}, f32[6,576]{1,0:T(8,128)}) all-reduce(f32[2,576]{1,0:T(2,128)S(1)} %pad_maximum_fusion.2, f32[1152]{0:T(1024)S(1)} %get-tuple-element.60, f32[2304]{0:T(1024)S(1)} %copy-done.54, ...), channel_id=1, replica_groups=mesh['dp'=16,'tensor'=2] {'dp'}, use_global_device_ids=true, to_apply=%region_25.26 | all-reduce | flops 9216 | bytes 73728 | tf_op jit(solution)/shard_map/psum | solution.py:237
  975.7 77.4 %reduce-scatter.27.cloned.1.call-done = f32[2304,72]{0,1:T(8,128)} async-done(((f32[2304,1152]{0,1:T(8,128)}), f32[2304,72]{0,1:T(8,128)}) %reduce-scatter.27.cloned.1.call-update) | async-done | bytes 663568 | tf_op jit(solution)/shard_map/reduce_scatter | solution.py:233
  1053.1 125.0 %reduce-scatter.25.cloned.1.call-done = f32[72,2304]{1,0:T(8,128)} async-done(((f32[1152,2304]{1,0:T(8,128)}), f32[72,2304]{1,0:T(8,128)}) %reduce-scatter.25.cloned.1.call-update) | async-done | bytes 663568 | tf_op jit(solution)/shard_map/reduce_scatter | solution.py:232
  1178.1 111.9 %reduce-scatter.23.cloned.1.call-done = f32[72,3,576]{2,0,1:T(8,128)} async-done(((f32[1152,3,576]{2,0,1:T(8,128)}), f32[72,3,576]{2,0,1:T(8,128)}) %reduce-scatter.23.cloned.1.call-update) | async-done | bytes 497680 | tf_op jit(solution)/shard_map/reduce_scatter | solution.py:230
  1290.0 190.2 %reduce-scatter.29.cloned.1.call-done = f32[72,6,576]{2,0,1:T(8,128)} async-done(((f32[1152,6,576]{2,0,1:T(8,128)}), f32[72,6,576]{2,0,1:T(8,128)}) %reduce-scatter.29.cloned.1.call-update) | async-done | bytes 995344 | tf_op jit(solution)/shard_map/reduce_scatter | solution.py:234
  (209 shorter events, 29.5 us)
Async XLA Ops:
  7.2 84.1 %all-gather.12.cloned.1.call-start = ((), (), s32[]{:S(2)}) async-start(), calls=%async_computation.10 | async-start | bytes 9400320 | tf_op jit(solution)/shard_map/all_gather | solution.py:52
  9.5 134.5 %all-gather.16.cloned.1.call-start = ((), (), s32[]{:S(2)}) async-start(), calls=%async_computation.12 | async-start | bytes 4700160 | tf_op jit(solution)/shard_map/all_gather | solution.py:48
  10.4 170.4 %all-gather.14.cloned.1.call-start = ((), (), s32[]{:S(2)}) async-start(), calls=%async_computation.11 | async-start | bytes 3538944 | tf_op jit(solution)/shard_map/all_gather | solution.py:97
  10.6 90.7 %copy-start.31 = (f32[512]{0:T(512)}, f32[512]{0:T(512)S(1)}, u32[]{:S(2)}) copy-start(f32[512]{0:T(512)S(1)} %broadcast_multiply_fusion.13) | copy-start | bytes 6148
  11.1 90.2 %copy-start.41 = (f32[512]{0:T(512)}, f32[512]{0:T(512)S(1)}, u32[]{:S(2)}) copy-start(f32[512]{0:T(512)S(1)} %add_rsqrt_fusion.1) | copy-start | bytes 6148
  11.8 84.3 %copy-start.37 = (f32[1,1152]{1,0:T(1,128)}, f32[1,1152]{1,0:T(1,128)S(1)}, u32[]{:S(2)}) copy-start(f32[1,1152]{1,0:T(1,128)S(1)} %get-tuple-element.63) | copy-start | bytes 13828
  91.3 4.8 copy-start.52
  101.3 195.0 %copy-start.29 = (f32[1152]{0:T(1024)}, f32[1152]{0:T(1024)S(1)}, u32[]{:S(2)}) copy-start(f32[1152]{0:T(1024)S(1)} %get-tuple-element.53) | copy-start | bytes 13828
  102.8 127.2 %all-gather.18.cloned.1.call-start = ((), (), s32[]{:S(2)}) async-start(), calls=%async_computation.13 | async-start | bytes 1566720 | tf_op jit(solution)/shard_map/all_gather | solution.py:49
  103.6 192.7 %reduce-scatter.15.cloned.1.call-start = ((), (), s32[]{:S(2)}) async-start(), calls=%async_computation.14 | async-start | bytes 7077888 | tf_op jit(solution)/shard_map/reduce_scatter | solution.py:121
  188.5 27.1 %copy-start.4 = (bf16[1024,3,576]{0,2,1:T(8,128)(2,1)}, bf16[1024,3,576]{0,2,1:T(8,128)(2,1)S(1)}, u32[]{:S(2)}) copy-start(bf16[1024,3,576]{0,2,1:T(8,128)(2,1)S(1)} %add_convert_fusion) | copy-start | bytes 10616836
  201.9 13.7 copy-start.21
  215.7 14.4 copy-start.27
  236.1 60.2 %copy-start.50 = (f32[1152]{0:T(1024)S(1)}, f32[1152]{0:T(1024)}, u32[]{:S(2)}) copy-start(f32[1152]{0:T(1024)} %param.19) | copy-start | bytes 13828
  236.2 119.4 %all-gather.22.cloned.1.call-start = ((), (), s32[]{:S(2)}) async-start(), calls=%async_computation.16 | async-start | bytes 5640192 | tf_op jit(solution)/shard_map/all_gather | solution.py:50
  238.0 154.4 %all-gather.20.cloned.1.call-start = ((), (), s32[]{:S(2)}) async-start(), calls=%async_computation.15 | async-start | bytes 3538944 | tf_op jit(solution)/shard_map/all_gather | solution.py:132
  301.3 150.5 %all-gather.24.cloned.1.call-start = ((), (), s32[]{:S(2)}) async-start(), calls=%async_computation.17 | async-start | bytes 5640192 | tf_op jit(solution)/shard_map/all_gather | solution.py:51
  302.2 149.6 %copy-start.58 = (f32[2304]{0:T(1024)S(1)}, f32[2304]{0:T(1024)}, u32[]{:S(2)}) copy-start(f32[2304]{0:T(1024)} %param.21) | copy-start | bytes 27652
  302.2 196.5 %reduce-scatter.17.cloned.1.call-start = ((), (), s32[]{:S(2)}) async-start(), calls=%async_computation.18 | async-start | bytes 3538944 | tf_op jit(solution)/shard_map/reduce_scatter | solution.py:140
  451.8 46.9 %copy-start.28 = (f32[1152]{0:T(1024)S(1)}, f32[1152]{0:T(1024)}, u32[]{:S(2)}) copy-start(f32[1152]{0:T(1024)} %get-tuple-element.48) | copy-start | bytes 13828
  451.8 46.9 %copy-start.39 = (f32[1152]{0:T(1024)S(1)}, f32[1152]{0:T(1024)}, u32[]{:S(2)}) copy-start(f32[1152]{0:T(1024)} %param.23) | copy-start | bytes 13828
  465.2 33.5 %copy-start.6 = (f32[512,1152]{1,0:T(8,128)S(1)}, f32[512,1152]{1,0:T(8,128)}, u32[]{:S(2)}) copy-start(f32[512,1152]{1,0:T(8,128)} %param.15) | copy-start | bytes 7077892
  465.3 73.1 %all-gather.26.cloned.1.call-start = ((), (), s32[]{:S(2)}) async-start(), calls=%async_computation.19 | async-start | bytes 3538944 | tf_op jit(solution)/shard_map/all_gather | solution.py:153
  502.1 124.8 %reduce-scatter.19.cloned.1.call-start = ((), (), s32[]{:S(2)}) async-start(), calls=%async_computation.20 | async-start | bytes 7077888 | tf_op jit(solution)/shard_map/reduce_scatter | solution.py:162
  566.7 60.2 %copy-start.3 = (f32[512,1152]{1,0:T(8,128)S(1)}, f32[512,1152]{1,0:T(8,128)}, u32[]{:S(2)}) copy-start(f32[512,1152]{1,0:T(8,128)} %copy-done.2) | copy-start | bytes 7077892
  566.7 63.6 %copy-start.17 = (bf16[512,1152]{1,0:T(8,128)(2,1)S(1)}, bf16[512,1152]{1,0:T(8,128)(2,1)}, u32[]{:S(2)}) copy-start(bf16[512,1152]{1,0:T(8,128)(2,1)} %reduce-scatter.17.cloned.1.call-done) | copy-start | bytes 3538948
  566.7 104.0 %all-gather.28.cloned.1.call-start = ((), (), s32[]{:S(2)}) async-start(), calls=%async_computation.21 | async-start | bytes 3538944 | tf_op jit(solution)/shard_map/all_gather | solution.py:174
  634.5 200.5 %reduce-scatter.21.cloned.1.call-start = ((), (), s32[]{:S(2)}) async-start(), calls=%async_computation.22 | async-start | bytes 7077888 | tf_op jit(solution)/shard_map/reduce_scatter | solution.py:207
  675.6 15.3 %copy-start.5 = (bf16[1024,3,576]{0,2,1:T(8,128)(2,1)S(1)}, bf16[1024,3,576]{0,2,1:T(8,128)(2,1)}, u32[]{:S(2)}) copy-start(bf16[1024,3,576]{0,2,1:T(8,128)(2,1)} %copy-done.4) | copy-start | bytes 10616836
  755.0 10.0 copy-start.11
  755.0 10.0 copy-start.13
  774.8 60.2 %copy-start.1 = (f32[512,1152]{1,0:T(8,128)S(1)}, f32[512,1152]{1,0:T(8,128)}, u32[]{:S(2)}) copy-start(f32[512,1152]{1,0:T(8,128)} %param.13) | copy-start | bytes 7077892
  774.8 60.2 %copy-start.26 = (f32[1152]{0:T(1024)S(1)}, f32[1152]{0:T(1024)}, u32[]{:S(2)}) copy-start(f32[1152]{0:T(1024)} %copy-done.25) | copy-start | bytes 13828
  774.9 60.2 %copy-start.32 = (f32[512]{0:T(512)S(1)}, f32[512]{0:T(512)}, u32[]{:S(2)}) copy-start(f32[512]{0:T(512)} %copy-done.31) | copy-start | bytes 6148
  774.9 60.2 %copy-start.42 = (f32[512]{0:T(512)S(1)}, f32[512]{0:T(512)}, u32[]{:S(2)}) copy-start(f32[512]{0:T(512)} %copy-done.41) | copy-start | bytes 6148
  774.9 112.2 %reduce-scatter.31.cloned.1.call-start = ((), (), s32[]{:S(2)}) async-start(), calls=%async_computation.27 | async-start | bytes 884736
  775.6 62.3 %copy-start.51 = (f32[1152]{0:T(1024)S(1)}, f32[1152]{0:T(1024)}, u32[]{:S(2)}) copy-start(f32[1152]{0:T(1024)} %param.19) | copy-start | bytes 13828
  843.1 132.6 %reduce-scatter.33.cloned.1.call-start = ((), (), s32[]{:S(2)}) async-start(), calls=%async_computation.28 | async-start | bytes 3133440
  848.9 204.2 %reduce-scatter.27.cloned.1.call-start = ((), (), s32[]{:S(2)}) async-start(), calls=%async_computation.25 | async-start | bytes 11280384 | tf_op jit(solution)/shard_map/reduce_scatter | solution.py:233
  862.1 316.0 %reduce-scatter.25.cloned.1.call-start = ((), (), s32[]{:S(2)}) async-start(), calls=%async_computation.24 | async-start | bytes 11280384 | tf_op jit(solution)/shard_map/reduce_scatter | solution.py:232
  874.3 415.7 %reduce-scatter.23.cloned.1.call-start = ((), (), s32[]{:S(2)}) async-start(), calls=%async_computation.23 | async-start | bytes 9400320 | tf_op jit(solution)/shard_map/reduce_scatter | solution.py:230
  886.4 593.8 %reduce-scatter.29.cloned.1.call-start = ((), (), s32[]{:S(2)}) async-start(), calls=%async_computation.26 | async-start | bytes 18800640 | tf_op jit(solution)/shard_map/reduce_scatter | solution.py:234
  897.7 9.4 copy-start.46
  897.7 9.5 copy-start.47
  897.7 16.8 %copy-start.23 = (f32[1,6,576]{2,1,0:T(8,128)S(1)}, f32[1,6,576]{2,1,0:T(8,128)}, u32[]{:S(2)}) copy-start(f32[1,6,576]{2,1,0:T(8,128)} %copy.52) | copy-start | bytes 41476
  897.7 16.8 %copy-start.54 = (f32[2304]{0:T(1024)S(1)}, f32[2304]{0:T(1024)}, u32[]{:S(2)}) copy-start(f32[2304]{0:T(1024)} %get-tuple-element.64) | copy-start | bytes 27652
  897.7 77.3 %copy-start.36 = (f32[1,1152]{1,0:T(1,128)S(1)}, f32[1,1152]{1,0:T(1,128)}, u32[]{:S(2)}) copy-start(f32[1,1152]{1,0:T(1,128)} %param.14) | copy-start | bytes 13828
  897.7 77.3 %copy-start.38 = (f32[1,1152]{1,0:T(1,128)S(1)}, f32[1,1152]{1,0:T(1,128)}, u32[]{:S(2)}) copy-start(f32[1,1152]{1,0:T(1,128)} %copy-done.37) | copy-start | bytes 13828
  (32 other events, 64.6 us)
Sparse Core Ops, SparseCore 0:
  10.8 80.4 all-gather.11
  94.1 49.9 all-gather.15
  146.1 34.5 all-gather.13
  183.3 39.3 all-gather.17
  236.3 59.9 reduce-scatter.14
  299.1 56.3 all-gather.21
  357.8 34.6 all-gather.19
  395.4 56.3 all-gather.23
  465.4 33.2 reduce-scatter.16
  502.2 36.0 all-gather.25
  566.8 59.9 reduce-scatter.18
  634.6 36.0 all-gather.27
  775.0 59.9 reduce-scatter.20
  843.2 15.2 reduce-scatter.30
  863.4 65.3 reduce-scatter.32
  933.8 119.2 reduce-scatter.26
  1058.1 119.9 reduce-scatter.24
  1183.3 106.7 reduce-scatter.22
  1294.8 185.3 reduce-scatter.28
where the time goes:
time: 1490 us
  waiting for transfers between devices  1080 us (72%)
  matrix products  220 us (15%)
  other arithmetic  82.8 us (6%)
  blocking collectives  72.4 us (5%)
  local copies, waits for them, and re-layouts  15.3 us (1%)
  between operations  15.1 us (1%)
    reduce_scatter x1, waiting for transfers between devices, body(): lax.psum_scatter(grad_ada, 'dp', scatter_dimension=0, tiled=True)  190 us
    reduce_scatter x1, waiting for transfers between devices, body(): lax.psum_scatter(grad_fc1, 'dp', scatter_dimension=0, tiled=True)  125 us
    reduce_scatter x1, waiting for transfers between devices, body(): lax.psum_scatter(grad_qkv_weight, 'dp', scatter_dimension=0, tiled=True)  112 us
    all_gather x1, waiting for transfers between devices, fetch(): lax.all_gather(ada_weight.astype(jnp.bfloat16), 'dp', axis=0, tiled=True)  79.5 us
    reduce_scatter x1, waiting for transfers between devices, body(): lax.psum_scatter(grad_fc2, 'dp', scatter_dimension=1, tiled=True)  77.4 us
    psum x1, blocking collectives, body(): lax.psum((qkv_bias_pair, tensor_totals[1], fc1_bias_part, tensor_totals[2...  60.6 us
    reduce_scatter x1, waiting for transfers between devices, body(): lax.psum_scatter(jnp.einsum('rf,df->rd', rows, w_fc1, preferred_element_t...  60.1 us
    reduce_scatter x1, waiting for transfers between devices, body(): lax.psum_scatter(jnp.einsum('rkf,dkf->rd', rows, w_qkv, preferred_element...  59.4 us
  transfers between devices with their start and end apart: 19, of which 16 were waited for; matrix products, arithmetic and copies ran while one was open for 9% of the time, Pallas kernels for 0%

commit v1 on v0

--- a/solution.py
+++ b/solution.py
@@ -1,6 +1,10 @@
+import functools
+
 import jax
 import jax.numpy as jnp
 from jax import lax
+from jax.experimental import pallas as pl
+from jax.experimental.pallas import tpu as pltpu
 from jax.sharding import PartitionSpec as P
 
 HEAD_DIM = 72
@@ -27,7 +31,7 @@
     return (grad - first - normed * second) * scaled
 
 
-def body(
+def general_body(
     latent_tokens,
     conditioning,
     out_grad,
@@ -254,6 +258,875 @@
     )
 
 
+LANES = 128
+LOG2E = 1.4426950408889634
+f32 = jnp.float32
+bf16 = jnp.bfloat16
+
+
+def fits(mesh):
+    return mesh.shape["tensor"] == 2 and mesh.shape["dp"] == 16
+
+
+def low(values):
+    return lax.reduce_precision(values, 8, 7).astype(bf16)
+
+
+def nn(a, b):
+    return lax.dot_general(a, b, (((1,), (0,)), ((), ())), preferred_element_type=f32)
+
+
+def nt(a, b):
+    return lax.dot_general(a, b, (((1,), (1,)), ((), ())), preferred_element_type=f32)
+
+
+def tn(a, b):
+    return lax.dot_general(a, b, (((0,), (0,)), ((), ())), preferred_element_type=f32)
+
+
+def window(head):
+    start = pl.multiple_of(((head * HEAD_DIM) // LANES) * LANES, LANES)
+    return start, head * HEAD_DIM - start
+
+
+def lane_mask(shape, first):
+    lane = lax.broadcasted_iota(jnp.int32, shape, 1)
+    return (lane >= first) & (lane < first + HEAD_DIM)
+
+
+def attend_kernel(q_ref, own_ref, oth_ref, o_ref, lse_ref, *, heads, block, pad, scale):
+    rows = q_ref.shape[0]
+    factor = scale * LOG2E
+    o_ref[...] = jnp.zeros_like(o_ref)
+
+    def one_head(h, carry):
+        at, first = window(h)
+
+        def one_block(i, inner):
+            r = pl.ds(pl.multiple_of(i * block, block), block)
+            mask = lane_mask((block, 2 * LANES), first)
+            q = q_ref[r, pl.ds(at, 2 * LANES)]
+            q = jnp.where(mask, q, jnp.zeros_like(q))
+            scores = [nt(ref[:, pl.ds(pad + at, 2 * LANES)], q) for ref in (own_ref, oth_ref)]
+            peak = functools.reduce(
+                jnp.maximum, [jnp.max(s, axis=0, keepdims=True) for s in scores]
+            )
+            peak = peak * factor
+            expo = [jnp.exp2(s * factor - peak) for s in scores]
+            total = sum(jnp.sum(e, axis=0, keepdims=True) for e in expo)
+            inverse = 1.0 / total
+            out = sum(
+                tn(ref[:, pl.ds(2 * pad + at, 2 * LANES)], (e * inverse).astype(bf16))
+                for ref, e in zip((own_ref, oth_ref), expo)
+            ).T
+            o_ref[r, pl.ds(at, 2 * LANES)] = jnp.where(
+                mask, out.astype(bf16), o_ref[r, pl.ds(at, 2 * LANES)]
+            )
+            lse_ref[pl.ds(h, 1), r] = peak + jnp.log2(total)
+            return inner
+
+        return lax.fori_loop(0, rows // block, one_block, carry)
+
+    lax.fori_loop(0, heads, one_head, 0)
+
+
+def attend(queries, own, oth, heads, pad):
+    rows = queries.shape[0]
+    flops = 4 * heads * rows * 2 * rows * 2 * LANES
+    return pl.pallas_call(
+        functools.partial(
+            attend_kernel, heads=heads, block=min(rows, 512), pad=pad, scale=HEAD_DIM**-0.5
+        ),
+        out_shape=(
+            jax.ShapeDtypeStruct((rows, pad), bf16),
+            jax.ShapeDtypeStruct((heads, rows), f32),
+        ),
+        cost_estimate=pl.CostEstimate(
+            flops=4 * flops, bytes_accessed=8 * rows * pad * 2, transcendentals=heads * rows * rows * 2
+        ),
+        compiler_params=pltpu.CompilerParams(vmem_limit_bytes=40 * 2**20),
+    )(queries, own, oth)
+
+
+def attend_back_kernel(
+    own_ref, oth_ref, gown_ref, goth_ref, lown_ref, loth_ref, down_ref, doth_ref, dk_ref, dv_ref,
+    *, heads, block, pad, scale,
+):
+    rows = own_ref.shape[0]
+    factor = scale * LOG2E
+    down_ref[...] = jnp.zeros_like(down_ref)
+    doth_ref[...] = jnp.zeros_like(doth_ref)
+
+    def one_head(h, carry):
+        at, first = window(h)
+        dk_ref[...] = jnp.zeros_like(dk_ref)
+        dv_ref[...] = jnp.zeros_like(dv_ref)
+        keys = [ref[:, pl.ds(pad + at, 2 * LANES)] for ref in (own_ref, oth_ref)]
+        values = [ref[:, pl.ds(2 * pad + at, 2 * LANES)] for ref in (own_ref, oth_ref)]
+        parts = ((own_ref, gown_ref, lown_ref, down_ref), (oth_ref, goth_ref, loth_ref, doth_ref))
+        for q_ref, g_ref, l_ref, d_ref in parts:
+
+            def one_block(i, inner):
+                r = pl.ds(pl.multiple_of(i * block, block), block)
+                mask = lane_mask((block, 2 * LANES), first)
+                q = q_ref[r, pl.ds(at, 2 * LANES)]
+                q = jnp.where(mask, q, jnp.zeros_like(q))
+                g = g_ref[r, pl.ds(at, 2 * LANES)]
+                g = jnp.where(mask, g, jnp.zeros_like(g))
+                lse = l_ref[pl.ds(h, 1), r]
+                probs = [jnp.exp2(nt(k, q) * factor - lse) for k in keys]
+                grad_p = [nt(v, g) for v in values]
+                delta = sum(jnp.sum(p * d, axis=0, keepdims=True) for p, d in zip(probs, grad_p))
+                grad_s = [(p * (d - delta)).astype(bf16) for p, d in zip(probs, grad_p)]
+                dq = sum(tn(k, s) for k, s in zip(keys, grad_s)).T * scale
+                d_ref[r, pl.ds(at, 2 * LANES)] = jnp.where(
+                    mask, dq.astype(bf16), d_ref[r, pl.ds(at, 2 * LANES)]
+                )
+                for j in range(2):
+                    dk_ref[j] += nn(grad_s[j], q)
+                    dv_ref[j] += nn(probs[j].astype(bf16), g)
+                return inner
+
+            lax.fori_loop(0, rows // block, one_block, 0)
+        mask = lane_mask((rows, 2 * LANES), first)
+        for j, d_ref in enumerate((down_ref, doth_ref)):
+            for lane, new in ((pad, dk_ref[j] * scale), (2 * pad, dv_ref[j])):
+                d_ref[:, pl.ds(lane + at, 2 * LANES)] = jnp.where(
+                    mask, new.astype(bf16), d_ref[:, pl.ds(lane + at, 2 * LANES)]
+                )
+        return carry
+
+    lax.fori_loop(0, heads, one_head, 0)
+
+
+def attend_back(own, oth, gown, goth, lown, loth, heads, pad):
+    rows = own.shape[0]
+    flops = 10 * heads * 4 * rows * rows * 2 * LANES
+    return pl.pallas_call(
+        functools.partial(
+            attend_back_kernel, heads=heads, block=min(rows, 512), pad=pad, scale=HEAD_DIM**-0.5
+        ),
+        out_shape=(jax.ShapeDtypeStruct((rows, 3 * pad), bf16),) * 2,
+        scratch_shapes=[pltpu.VMEM((2, rows, 2 * LANES), f32)] * 2,
+        cost_estimate=pl.CostEstimate(
+            flops=flops, bytes_accessed=16 * rows * pad * 2, transcendentals=heads * rows * rows * 4
+        ),
+        compiler_params=pltpu.CompilerParams(vmem_limit_bytes=56 * 2**20),
+    )(own, oth, gown, goth, lown, loth)
+
+
+GELU = 0.7978845608028654
+
+
+def feed_kernel(m_ref, g_ref, w1_ref, w2_ref, b_ref, act_ref, gp_ref, h_ref, acc_ref, *, steps):
+    i = pl.program_id(0)
+
+    @pl.when(i == 0)
+    def _():
+        acc_ref[...] = jnp.zeros_like(acc_ref)
+
+    pre = nn(m_ref[...], w1_ref[...]) + b_ref[...]
+    grad_act = nn(g_ref[...], w2_ref[...])
+    square = pre * pre
+    gate = 1.0 / (1.0 + jnp.exp((-2.0 * GELU) * pre * (1.0 + 0.044715 * square)))
+    act_ref[...] = (pre * gate).astype(bf16)
+    slope = gate + pre * gate * (1.0 - gate) * ((2.0 * GELU) * (1.0 + (3.0 * 0.044715) * square))
+    grad_pre = (grad_act * slope).astype(bf16)
+    gp_ref[...] = grad_pre
+    acc_ref[...] += nt(grad_pre, w1_ref[...])
+
+    @pl.when(i == steps - 1)
+    def _():
+        h_ref[...] = acc_ref[...].astype(h_ref.dtype)
+
+
+def feed(m, g, weights, bias, out_dtype):
+    rows, depth = m.shape
+    hidden = weights.shape[1] // 2
+    steps = 3 if hidden % (3 * LANES) == 0 else 1
+    chunk = hidden // steps
+    whole = pl.BlockSpec((rows, depth), lambda i: (0, 0))
+    first = pl.BlockSpec((depth, chunk), lambda i: (0, i))
+    second = pl.BlockSpec((depth, chunk), lambda i: (0, i + steps))
+    tall = pl.BlockSpec((rows, chunk), lambda i: (0, i))
+    return pl.pallas_call(
+        functools.partial(feed_kernel, steps=steps),
+        grid=(steps,),
+        in_specs=[whole, whole, first, second, pl.BlockSpec((1, chunk), lambda i: (0, i))],
+        out_specs=[tall, tall, whole],
+        out_shape=(
+            jax.ShapeDtypeStruct((rows, hidden), bf16),
+            jax.ShapeDtypeStruct((rows, hidden), bf16),
+            jax.ShapeDtypeStruct((rows, depth), out_dtype),
+        ),
+        scratch_shapes=[pltpu.VMEM((rows, depth), f32)],
+        cost_estimate=pl.CostEstimate(
+            flops=12 * rows * depth * hidden,
+            bytes_accessed=4 * depth * hidden + 8 * rows * depth + 4 * rows * hidden,
+            transcendentals=rows * hidden,
+        ),
+        compiler_params=pltpu.CompilerParams(vmem_limit_bytes=48 * 2**20),
+    )(m, g, weights, weights, bias)
+
+
+def outer_kernel(
+    core_ref, lown_ref, loth_ref, rown_ref, roth_ref, keep_ref, send_ref, sum_ref, turned_ref,
+    *, lines, block,
+):
+    core = core_ref[0]
+    rows = lown_ref.shape[0]
+
+    @pl.when(pl.program_id(0) == 0)
+    def _():
+        for j, ref in enumerate((lown_ref, loth_ref)):
+            turned = ref[...].astype(f32).T
+            for z in range(lines):
+                for x in range(2):
+                    for c in range(2):
+                        b = (z * 2 + x) * 2 + c
+                        turned_ref[c, pl.ds((x * lines + z) * block, block), pl.ds(j * rows, rows)] = (
+                            turned[b * block : (b + 1) * block].astype(bf16)
+                        )
+
+    for out_ref, which in ((send_ref, 1 - core), (keep_ref, core)):
+        made = nn(turned_ref[which, :, pl.ds(0, rows)], rown_ref[...])
+        made += nn(turned_ref[which, :, pl.ds(rows, rows)], roth_ref[...])
+        out_ref[...] = made.reshape(out_ref.shape)
+    ones = jnp.ones((8, rows), bf16)
+    sum_ref[...] = nn(ones, rown_ref[...]) + nn(ones, roth_ref[...])
+
+
+def outer(core, left_own, left_oth, right_own, right_oth, block):
+    rows, depth = left_own.shape
+    wide = right_own.shape[1]
+    lines = depth // block // 4
+    steps = next(n for n in (3, 2, 1) if wide % (n * LANES) == 0)
+    chunk = wide // steps
+    whole = pl.BlockSpec((rows, depth), lambda i, c: (0, 0))
+    tall = pl.BlockSpec((rows, chunk), lambda i, c: (0, i))
+    out = pl.BlockSpec((2, lines, block, chunk), lambda i, c: (0, 0, 0, i))
+    return pl.pallas_call(
+        functools.partial(outer_kernel, lines=lines, block=block),
+        grid_spec=pltpu.PrefetchScalarGridSpec(
+            num_scalar_prefetch=1,
+            grid=(steps,),
+            in_specs=[whole, whole, tall, tall],
+            out_specs=[out, out, pl.BlockSpec((8, chunk), lambda i, c: (0, i))],
+            scratch_shapes=[pltpu.VMEM((2, depth // 2, 2 * rows), bf16)],
+        ),
+        out_shape=(jax.ShapeDtypeStruct((2, lines, block, wide), f32),) * 2
+        + (jax.ShapeDtypeStruct((8, wide), f32),),
+        cost_estimate=pl.CostEstimate(
+            flops=8 * rows * depth * wide,
+            bytes_accessed=4 * depth * wide + 4 * rows * (depth + wide),
+            transcendentals=0,
+        ),
+        compiler_params=pltpu.CompilerParams(vmem_limit_bytes=48 * 2**20),
+    )(core, left_own, left_oth, right_own, right_oth)
+
+
+def turn_kernel(h_ref, got_ref, mid_ref, grad_ref, branch_ref, scale_ref, gate_ref, out_ref, z_ref, sum_ref):
+    h = h_ref[...] + got_ref[...].astype(f32)
+    normed, rscale = normalize(mid_ref[...])
+    mid_grad = grad_ref[...] + norm_back(h * (1.0 + scale_ref[...]), normed, rscale)
+    out_ref[...] = mid_grad
+    z = (gate_ref[...] * mid_grad).astype(bf16)
+    z_ref[...] = z
+
+    @pl.when(pl.program_id(0) == 0)
+    def _():
+        sum_ref[...] = jnp.zeros_like(sum_ref)
+
+    for j, values in enumerate((mid_grad * branch_ref[...], h, h * normed, z.astype(f32))):
+        sum_ref[pl.ds(j, 1), :] += jnp.sum(values, axis=0, keepdims=True)
+
+
+def turn(h_own, h_got, middle, out_grad, branch, scale, gate):
+    rows, depth = middle.shape
+    tile = min(rows, 128)
+    part = pl.BlockSpec((tile, depth), lambda i: (i, 0))
+    line = pl.BlockSpec((1, depth), lambda i: (0, 0))
+    return pl.pallas_call(
+        turn_kernel,
+        grid=(rows // tile,),
+        in_specs=[part] * 5 + [line] * 2,
+        out_specs=[part, part, pl.BlockSpec((8, depth), lambda i: (0, 0))],
+        out_shape=(
+            jax.ShapeDtypeStruct((rows, depth), f32),
+            jax.ShapeDtypeStruct((rows, depth), bf16),
+            jax.ShapeDtypeStruct((8, depth), f32),
+        ),
+        cost_estimate=pl.CostEstimate(
+            flops=40 * rows * depth, bytes_accessed=24 * rows * depth, transcendentals=rows
+        ),
+        compiler_params=pltpu.CompilerParams(vmem_limit_bytes=32 * 2**20),
+    )(h_own, h_got, middle, out_grad, branch, scale.reshape(1, -1), gate.reshape(1, -1))
+
+
+def peers(n_dp):
+    me, side = lax.axis_index("dp"), lax.axis_index("tensor")
+    n_z = n_dp // 4
+    z, x, c = me // 4, (me // 2) % 2, me % 2
+    across = (me, 1 - side)
+    core = (z * 4 + x * 2 + 1 - c, side)
+    beside = (z * 4 + (1 - x) * 2 + c, side)
+    lines = [(lax.rem(z + s, n_z) * 4 + x * 2 + c, side) for s in range(1, n_z)]
+    return (me, z, x, c), across, core, beside, lines
+
+
+def greet(partners):
+    barrier = pltpu.get_barrier_semaphore()
+    for partner in partners:
+        pl.semaphore_signal(barrier, inc=1, device_id=partner, device_id_type=pl.DeviceIdType.MESH)
+    pl.semaphore_wait(barrier, len(partners))
+
+
+def close_kernel(
+    aown_ref, aoth_ref, down_ref, doth_ref, mine_ref, other_ref, cond_ref, scale_ref,
+    w_any, x_any, mid_any, zown_any, zoth_any, oown_any, ooth_any, ada_any,
+    tokens_ref, grads_ref, gada_ref, total_ref, row_ref,
+    w_ref, x_ref, mid_ref, z_ref, o_ref, ada_ref,
+    turned_ref, part_ref, got_ref, xgot_ref, zgot_ref, hsend_ref, hgot_ref, hown_ref,
+    rows_ref, rgot_ref, all_ref, cpart_ref, cswap_ref, parts_ref,
+    load_sem, send_sem, recv_sem,
+    *, n_dp, n_mods, n_shared, pad,
+):
+    (me, z, x, c), across, core, beside, lines = peers(n_dp)
+    n_z = n_dp // 4
+    side = lax.axis_index("tensor")
+    loads = [
+        pltpu.make_async_copy(source, target, load_sem.at[k])
+        for k, (source, target) in enumerate(
+            (
+                (w_any, w_ref),
+                (zown_any, z_ref.at[0]),
+                (zoth_any, z_ref.at[1]),
+                (oown_any, o_ref.at[0]),
+                (ooth_any, o_ref.at[1]),
+                (x_any, x_ref),
+                (mid_any, mid_ref),
+                (ada_any, ada_ref),
+            )
+        )
+    ]
+    for load in loads:
+        load.start()
+    greet([across, core, beside] + lines)
+
+    rows, depth = aown_ref.shape
+    width = mine_ref.shape[1]
+    block = got_ref.shape[3]
+    n_parts = part_ref.shape[0]
+    tile = min(rows, 128)
+
+    def link(source, target, to, k):
+        return pltpu.make_async_remote_copy(
+            src_ref=source, dst_ref=target, send_sem=send_sem.at[k], recv_sem=recv_sem.at[k],
+            device_id=to, device_id_type=pl.DeviceIdType.MESH,
+        )
+
+    def core_link(k):
+        return link(part_ref.at[k], got_ref.at[k], core, k)
+
+    def x_link(k):
+        return link(got_ref.at[k, 1 - x], xgot_ref.at[k], beside, n_parts + k)
+
+    def z_link(k, s):
+        to = lax.rem(z + s + 1, n_z)
+        at = 2 * n_parts + k * (n_z - 1) + s
+        return link(got_ref.at[k, x, to], zgot_ref.at[k, s], lines[s], at)
+
+    first_sum = (n_z + 1) * n_parts
+    half = link(hsend_ref, hgot_ref, across, first_sum)
+
+    def turn_over(refs):
+        for j, read in enumerate(refs):
+            turned = read().astype(f32).T
+            for zz in range(n_z):
+                for xx in range(2):
+                    for cc in range(2):
+                        b = (zz * 2 + xx) * 2 + cc
+                        at = pl.ds((xx * n_z + zz) * block, block)
+                        turned_ref[cc, at, pl.ds(j * rows, rows)] = turned[
+                            b * block : (b + 1) * block
+                        ].astype(bf16)
+
+    def product(which, right_own, right_oth):
+        made = nn(turned_ref[which, :, pl.ds(0, rows)], right_own)
+        made += nn(turned_ref[which, :, pl.ds(rows, rows)], right_oth)
+        return made.reshape(got_ref.shape[1:])
+
+    def columns(k):
+        at = pl.ds(pl.multiple_of(k * pad, LANES), pad)
+        return down_ref[:, at], doth_ref[:, at]
+
+    def to_core(k, carry):
+        part_ref[k] = product(1 - c, *columns(k))
+        core_link(k).start()
+        return carry
+
+    def to_beside(k, carry):
+        core_link(k).wait_recv()
+        got_ref[k] += product(c, *columns(k))
+        x_link(k).start()
+        return carry
+
+    def to_lines(k, carry):
+        x_link(k).wait_recv()
+        got_ref[k, x] += xgot_ref[k]
+        for s in range(n_z - 1):
+            z_link(k, s).start()
+        return carry
+
+    turn_over((lambda: aown_ref[...], lambda: aoth_ref[...]))
+    lax.fori_loop(0, 3, to_core, 0)
+    lax.fori_loop(0, 3, to_beside, 0)
+
+    loads[0].wait()
+
+    def h_other(i, carry):
+        r = pl.ds(pl.multiple_of(i * tile, tile), tile)
+        hsend_ref[r, :] = nt(doth_ref[r, :], w_ref[...]).astype(bf16)
+        return carry
+
+    lax.fori_loop(0, rows // tile, h_other, 0)
+    half.start()
+
+    for load in loads[1:5]:
+        load.wait()
+    turn_over((lambda: z_ref[0], lambda: z_ref[1]))
+    part_ref[3] = product(1 - c, o_ref[0], o_ref[1])
+    core_link(3).start()
+
+    def h_own(i, carry):
+        r = pl.ds(pl.multiple_of(i * tile, tile), tile)
+        hown_ref[r, :] = nt(down_ref[r, :], w_ref[...])
+        return carry
+
+    lax.fori_loop(0, rows // tile, h_own, 0)
+    ones = jnp.ones((8, rows), bf16)
+    d_sums = nn(ones, down_ref[...]) + nn(ones, doth_ref[...])
+    core_link(3).wait_recv()
+    got_ref[3] += product(c, o_ref[0], o_ref[1])
+    x_link(3).start()
+    to_lines(0, 0)
+
+    for load in loads[5:]:
+        load.wait()
+    half.wait_recv()
+
+    def last_norm(i, carry):
+        r = pl.ds(pl.multiple_of(i * tile, tile), tile)
+        h = hown_ref[r, :] + hgot_ref[r, :].astype(f32)
+        normed, rscale = normalize(x_ref[r, :])
+        tokens_ref[r, :] = mid_ref[r, :] + norm_back(h * (1.0 + scale_ref[...]), normed, rscale)
+        shift_sum, scale_sum = carry
+        shift_sum += jnp.sum(h, axis=0, keepdims=True)
+        scale_sum += jnp.sum(h * normed, axis=0, keepdims=True)
+        return shift_sum, scale_sum
+
+    none = jnp.zeros((1, depth), f32)
+    late = lax.fori_loop(0, rows // tile, last_norm, (none, none))
+
+    rows_ref[0] = mine_ref[...]
+    rows_ref[1] = other_ref[...]
+    for j, values in enumerate(late):
+        low_half, high_half = values[:, :width], values[:, width:]
+        rows_ref[0, pl.ds(j, 1), :] = jnp.where(side == 0, low_half, high_half)
+        rows_ref[1, pl.ds(j, 1), :] = jnp.where(side == 0, high_half, low_half)
+    for j, at in ((0, 0), (1, 2 * pad)):
+        rows_ref[0, pl.ds(n_mods + j, 1), :] = d_sums[:1, at : at + width]
+    first_sum += 1
+    swap_rows = link(rows_ref.at[1], rgot_ref, across, first_sum)
+    swap_rows.start()
+    to_lines(1, 0)
+    swap_rows.wait()
+    row = lax.broadcasted_iota(jnp.int32, mine_ref.shape, 0)
+    shared = (row < n_mods) | (row >= mine_ref.shape[0] - n_shared)
+    all_ref[z, x, c] = rows_ref[0] + jnp.where(shared, rgot_ref[...], 0.0)
+
+    def spread(ref, first):
+        copy = link(ref.at[z, x, c], ref.at[z, x, c], core, first)
+        copy.start()
+        copy.wait()
+        copy = link(ref.at[z, x], ref.at[z, x], beside, first + 1)
+        copy.start()
+        copy.wait()
+        copies = [link(ref.at[z], ref.at[z], to, first + 2 + s) for s, to in enumerate(lines)]
+        for copy in copies:
+            copy.start()
+        for copy in copies:
+            copy.wait()
+
+    spread(all_ref, first_sum + 1)
+    to_lines(2, 0)
+    everything = all_ref[...].reshape((n_dp,) + mine_ref.shape)
+    total_ref[...] = jnp.sum(everything, axis=0)
+    cond = cond_ref[...]
+    part = jnp.zeros(cond.shape, f32)
+    for j in range(n_mods):
+        grad = everything[:, j, :]
+        gada_ref[j] = lax.dot_general(
+            cond, grad, (((0,), (0,)), ((), ())),
+            precision=highest_precision_mode, preferred_element_type=f32,
+        )
+        part += lax.dot_general(
+            grad, ada_ref[j].astype(f32), (((1,), (1,)), ((), ())),
+            precision=highest_precision_mode, preferred_element_type=f32,
+        )
+    cpart_ref[...] = part
+    swap_part = link(cpart_ref, cswap_ref, across, first_sum + n_z + 2)
+    swap_part.start()
+    swap_part.wait()
+    whole = cpart_ref[...] + cswap_ref[...]
+    for l in range(n_dp):
+        parts_ref[z, x, c, l] = whole[l : l + 1]
+    spread(parts_ref, first_sum + n_z + 3)
+    for p in range(n_dp):
+        row_ref[pl.ds(p, 1), :] = parts_ref[p // 4, (p // 2) % 2, p % 2, me]
+
+    to_lines(3, 0)
+
+    def finish(k, carry):
+        total = got_ref[k, x, z]
+        for s in range(n_z - 1):
+            z_link(k, s).wait_recv()
+            total += zgot_ref[k, s]
+        grads_ref[k] = total
+        return carry
+
+    lax.fori_loop(0, n_parts, finish, 0)
+    half.wait_send()
+
+    def sent(k, carry):
+        core_link(k).wait_send()
+        x_link(k).wait_send()
+        for s in range(n_z - 1):
+            z_link(k, s).wait_send()
+        return carry
+
+    lax.fori_loop(0, n_parts, sent, 0)
+
+
+def close(
+    a_own, a_oth, d_own, d_oth, mine, other, cond, scale, w_qkv, tokens, mid_grad,
+    z_own, z_oth, o_own, o_oth, ada, n_shared,
+):
+    n_dp = lax.axis_size("dp")
+    n_z = n_dp // 4
+    n_mods, block, width = ada.shape
+    rows, depth = tokens.shape
+    pad = o_own.shape[1]
+    n_rows = mine.shape[0]
+    n_parts = 4
+    n_links = (n_z + 1) * n_parts + 1 + 2 * (n_z + 2)
+    vmem = pl.BlockSpec(memory_space=pltpu.VMEM)
+    return pl.pallas_call(
+        functools.partial(close_kernel, n_dp=n_dp, n_mods=n_mods, n_shared=n_shared, pad=pad),
+        out_shape=(
+            jax.ShapeDtypeStruct((rows, depth), f32),
+            jax.ShapeDtypeStruct((n_parts, block, pad), f32),
+            jax.ShapeDtypeStruct((n_mods, block, width), f32),
+            jax.ShapeDtypeStruct((n_rows, width), f32),
+            jax.ShapeDtypeStruct((n_dp, block), f32),
+        ),
+        in_specs=[vmem] * 8 + [pl.BlockSpec(memory_space=pl.ANY)] * 8,
+        out_specs=[vmem] * 5,
+        scratch_shapes=[
+            pltpu.VMEM(w_qkv.shape, bf16),
+            pltpu.VMEM((rows, depth), f32),
+            pltpu.VMEM((rows, depth), f32),
+            pltpu.VMEM((2, rows, depth), bf16),
+            pltpu.VMEM((2, rows, pad), bf16),
+            pltpu.VMEM(ada.shape, bf16),
+            pltpu.VMEM((2, depth // 2, 2 * rows), bf16),
+            pltpu.VMEM((n_parts, 2, n_z, block, pad), f32),
+            pltpu.VMEM((n_parts, 2, n_z, block, pad), f32),
+            pltpu.VMEM((n_parts, n_z, block, pad), f32),
+            pltpu.VMEM((n_parts, n_z - 1, block, pad), f32),
+            pltpu.VMEM((rows, depth), bf16),
+            pltpu.VMEM((rows, depth), bf16),
+            pltpu.VMEM((rows, depth), f32),
+            pltpu.VMEM((2, n_rows, width), f32),
+            pltpu.VMEM((n_rows, width), f32),
+            pltpu.VMEM((n_z, 2, 2, n_rows, width), f32),
+            pltpu.VMEM((n_dp, block), f32),
+            pltpu.VMEM((n_dp, block), f32),
+            pltpu.VMEM((n_z, 2, 2, n_dp, 1, block), f32),
+            pltpu.SemaphoreType.DMA((8,)),
+            pltpu.SemaphoreType.DMA((n_links,)),
+            pltpu.SemaphoreType.DMA((n_links,)),
+        ],
+        cost_estimate=pl.CostEstimate(
+            flops=60 * 10**9, bytes_accessed=100 * 10**6, transcendentals=0
+        ),
+        compiler_params=pltpu.CompilerParams(
+            collective_id=0, has_side_effects=True, vmem_limit_bytes=60 * 2**20
+        ),
+    )(
+        a_own, a_oth, d_own, d_oth, mine, other, cond, scale.reshape(1, -1),
+        w_qkv, tokens, mid_grad, z_own, z_oth, o_own, o_oth, ada,
+    )
+
+
+def after(value, *others):
+    return lax.optimization_barrier((value,) + others)[0]
+
+
+TOP = 32768.0
+
+
+def fast_body(
+    latent_tokens,
+    conditioning,
+    out_grad,
+    qkv_weight,
+    qkv_bias,
+    proj_weight,
+    proj_bias,
+    first_layer_weight,
+    fc1_bias,
+    fc2_weight,
+    second_layer_bias,
+    ada_weight,
+    ada_bias,
+):
+    n_dp = lax.axis_size("dp")
+    n_z = n_dp // 4
+    me = lax.axis_index("dp")
+    side = lax.axis_index("tensor")
+    core, at_x, at_z = me % 2, (me // 2) % 2, me // 4
+    rows, width_full = latent_tokens.shape
+    block, _, width = qkv_weight.shape
+    heads = width // HEAD_DIM
+    pad = -(-width // LANES) * LANES
+
+    def swap(values):
+        return lax.ppermute(values, "tensor", [(0, 1), (1, 0)])
+
+    def flip(values, bit):
+        return lax.ppermute(values, "dp", [(i, i ^ bit) for i in range(n_dp)])
+
+    def shift(values, step):
+        return lax.ppermute(values, "dp", [(i, (i + 4 * step) % n_dp) for i in range(n_dp)])
+
+    def place(pieces, spots):
+        out = jnp.zeros((len(pieces),) + pieces[0].shape, pieces[0].dtype)
+        for piece, spot in zip(pieces, spots):
+            out = lax.dynamic_update_index_in_dim(out, piece, spot, 0)
+        return out
+
+    def pair(mine, other, bit):
+        return jnp.where(bit == 0, jnp.stack([mine, other]), jnp.stack([other, mine]))
+
+    def along_z(values):
+        pieces = [values] + [shift(values, s) for s in range(1, n_z)]
+        return place(pieces, [(at_z - s) % n_z for s in range(n_z)])
+
+    def in_order(both, shape):
+        both = both.reshape((2, 2, n_z) + shape)
+        return jnp.transpose(both, (2, 1, 0) + tuple(range(3, both.ndim))).reshape((n_dp,) + shape)
+
+    def gather(values):
+        lines = along_z(values)
+        planes = place([lines, flip(lines, 2)], [at_x, 1 - at_x])
+        both = place([planes, flip(planes, 1)], [core, 1 - core])
+        return in_order(both, values.shape)
+
+    def pick(array, spot, axis):
+        return lax.dynamic_index_in_dim(array, spot, axis, keepdims=False)
+
+    def scatter_sum(values):
+        parts = values.reshape((n_z, 2, 2) + values.shape[1:])
+        parts = pick(parts, core, 2) + flip(pick(parts, 1 - core, 2), 1)
+        parts = pick(parts, at_x, 1) + flip(pick(parts, 1 - at_x, 1), 2)
+        total = pick(parts, at_z, 0)
+        for s in range(1, n_z):
+            total = total + shift(pick(parts, (at_z + s) % n_z, 0), s)
+        return total
+
+    def narrow(part, bound):
+        return (part * (TOP / bound)).astype(jnp.float16)
+
+    def wide(part, bound):
+        return part.astype(f32) * (bound * (1.0 / TOP))
+
+    def biggest_over_dp(values):
+        values = jnp.maximum(values, flip(values, 1))
+        values = jnp.maximum(values, flip(values, 2))
+        others = [shift(values, s) for s in range(1, n_z)]
+        return functools.reduce(jnp.maximum, others, values)
+
+    def total_over_dp(values):
+        values = values + flip(values, 1)
+        values = values + flip(values, 2)
+        return jnp.sum(along_z(values), axis=0)
+
+    def halves(mine, other, axis):
+        first = jnp.where(side == 0, mine, other)
+        second = jnp.where(side == 0, other, mine)
+        return jnp.concatenate([first, second], axis=axis)
+
+    def pad_lanes(values):
+        return jnp.pad(values, [(0, 0)] * (values.ndim - 1) + [(0, pad - width)])
+
+    def biggest(*pieces):
+        return functools.reduce(jnp.maximum, [jnp.max(jnp.abs(v.astype(f32))) for v in pieces])
+
+    out_top = biggest(out_grad).reshape(1)
+    out_top = jnp.maximum(out_top, swap(out_top))
+    normed_one, rscale_one = normalize(latent_tokens)
+
+    def full_weight(shard):
+        return lax.all_gather(shard, "dp", axis=0, tiled=True)
+
+    first = [
+        pad_lanes(qkv_weight.astype(bf16)).reshape(block, 3 * pad),
+        pad_lanes(proj_weight.astype(bf16).T),
+    ]
+    w_first = full_weight(jnp.concatenate(first, axis=1))
+    w_qkv, w_proj = w_first[:, : 3 * pad], w_first[:, 3 * pad :]
+    second = [first_layer_weight.astype(bf16), fc2_weight.astype(bf16).T]
+    w_second = full_weight(jnp.concatenate(second, axis=1))
+    hidden = first_layer_weight.shape[1]
+    w_fc2 = w_second[:, hidden:]
+
+    silu_cond, silu_pull = jax.vjp(jax.nn.silu, conditioning)
+    cond_all = gather(low(silu_cond)).reshape(n_dp, width_full)
+    cond_mine = lax.dynamic_slice_in_dim(cond_all, me * block, block, 1)
+    w_ada = ada_weight.astype(bf16).reshape(block, 6 * width)
+    mods_half = scatter_sum(nn(cond_mine, w_ada)).reshape(6, width) + ada_bias
+    mods = halves(mods_half, swap(mods_half), 1)
+    shift_one, scale_one, gate_one, shift_two, scale_two, gate_two = [mods[j] for j in range(6)]
+
+    tokens = float(n_dp * SEQ)
+    tiny = 1e-30
+    norm = 1.01 * width_full**0.5
+    bounds = jnp.concatenate(
+        [
+            out_top * biggest(gate_two),
+            (biggest(scale_two) + biggest(shift_two) + 1.0).reshape(1) * norm,
+        ]
+    )
+    bounds = biggest_over_dp(bounds)
+    act_bound = bounds[1] * (0.1875 * norm) + 3.0
+    gp_bound = bounds[0] * (1.2 * 0.09375 * width_full)
+    fc2_bound = bounds[0] * act_bound * (1.01 * tokens) + tiny
+    fc1_bound = bounds[1] * gp_bound * (1.01 * tokens) + tiny
+    v_bound = (biggest(scale_one) + biggest(shift_one) + 1.0) * (norm * 0.1875 * norm) + 1.25
+    p_bound = v_bound * (1.01 * 0.75 * width)
+
+    a_own = low(normed_one * (1.0 + scale_one) + shift_one)
+    a_oth = swap(a_own)
+    g_own = low(gate_two * out_grad)
+    g_oth = swap(after(g_own, a_own))
+    bias = pad_lanes(jnp.stack([qkv_bias[0], jnp.zeros_like(qkv_bias[0]), qkv_bias[1]]))
+    bias = bias.reshape(3 * pad)
+    qkv_own = (nn(after(a_own, bounds), w_qkv) + bias).astype(bf16)
+    qkv_oth = (nn(a_oth, w_qkv) + bias).astype(bf16)
+    o_oth, lse_oth = attend(qkv_oth, qkv_own, qkv_oth, heads, pad)
+    p_send = narrow(nt(o_oth, w_proj), p_bound)
+    part_oth = wide(swap(p_send), p_bound)
+    o_own, lse_own = attend(after(qkv_own, p_send), qkv_own, qkv_oth, heads, pad)
+    branch_one = nt(o_own, w_proj) + part_oth + proj_bias
+    middle = latent_tokens + gate_one * branch_one
+    normed_two, rscale_two = normalize(middle)
+
+    m_own = low(normed_two * (1.0 + scale_two) + shift_two)
+    m_oth = swap(m_own)
+    hidden_bias = fc1_bias.reshape(1, -1)
+    act_own, gp_own, h_own = feed(m_own, g_own, w_second, hidden_bias, f32)
+    act_oth, gp_oth, h_send = feed(m_oth, after(g_oth, m_own), w_second, hidden_bias, bf16)
+    h_recv = swap(h_send)
+
+    this_core = core.astype(jnp.int32).reshape(1)
+    kept_fc2, sent_fc2, _ = outer(
+        this_core, g_own, g_oth, after(act_own, h_send), act_oth, block
+    )
+    got_fc2 = flip(sent_fc2, 1)
+    kept_fc1, sent_fc1, fc1_sums = outer(
+        this_core, m_own, m_oth, after(gp_own, sent_fc2), gp_oth, block
+    )
+    got_fc1 = flip(sent_fc1, 1)
+
+    def x_halves(kept, got, bound):
+        mine = pick(kept, at_x, 0) + pick(got, at_x, 0)
+        other = pick(kept, 1 - at_x, 0) + pick(got, 1 - at_x, 0)
+        return mine, narrow(other, bound)
+
+    def z_sent(parts, bound):
+        return [narrow(pick(parts, (at_z + s) % n_z, 0), bound) for s in range(1, n_z)]
+
+    fc2_mine, fc2_send = x_halves(kept_fc2, after(got_fc2, kept_fc1), fc2_bound)
+    fc2_x = flip(fc2_send, 2)
+    mid_grad, z_own, turned = turn(
+        h_own, after(h_recv, fc2_send), middle, out_grad, branch_one, scale_two, gate_one
+    )
+    z_oth = swap(z_own)
+    fc1_mine, fc1_send = x_halves(kept_fc1, after(got_fc1, z_own), fc1_bound)
+    b_send = nt(after(act_oth, fc1_send), w_fc2).astype(bf16)
+    b_own = nt(after(act_own, b_send), w_fc2)
+    go_own = nn(after(z_own, b_own), w_proj).astype(bf16)
+    fc2_parts = fc2_mine + wide(after(fc2_x, go_own), fc2_bound)
+    fc2_z = z_sent(fc2_parts, fc2_bound)
+    fc1_x = flip(after(fc1_send, fc2_z[0]), 2)
+    go_oth = nn(after(z_oth, *fc2_z), w_proj).astype(bf16)
+    b_oth = swap(after(b_send, go_oth)).astype(f32)
+    d_own, d_oth = attend_back(
+        qkv_own, qkv_oth, go_own, go_oth, lse_own, lse_oth, heads, pad
+    )
+    fc1_parts = fc1_mine + wide(after(fc1_x, d_own), fc1_bound)
+    fc1_z = z_sent(fc1_parts, fc1_bound)
+
+    def z_total(parts, sent, bound):
+        return pick(parts, at_z, 0) + sum(
+            wide(shift(part, s + 1), bound) for s, part in enumerate(sent)
+        )
+
+    grad_fc1 = z_total(fc1_parts, fc1_z, fc1_bound)
+    grad_fc2 = z_total(fc2_parts, fc2_z, fc2_bound).T
+    branch_two = b_own + b_oth + second_layer_bias
+    layer_out = middle + gate_two * branch_two
+
+    sums = functools.partial(jnp.sum, axis=0)
+    empty = jnp.zeros((2, width_full), f32)
+    mods_sums = jnp.stack([turned[0], turned[1], turned[2], sums(out_grad * branch_two)])
+    mods_sums = jnp.concatenate([empty, mods_sums]).reshape(6, 2, width)
+    apart = jnp.concatenate([jnp.zeros((2, width), f32), fc1_sums[0].reshape(-1, width)])
+    shared = jnp.stack([turned[3], sums(g_own.astype(f32))]).reshape(-1, width)
+    mine = jnp.concatenate([pick(mods_sums, side, 1), apart, shared])
+    other = jnp.concatenate([pick(mods_sums, 1 - side, 1), apart, shared])
+    ada = jnp.transpose(w_ada.reshape(block, 6, width), (1, 0, 2))
+    tokens_grad, grads, grad_ada, totals, cond_row = close(
+        a_own, a_oth, after(d_own, *fc1_z), d_oth, mine, other, cond_mine.astype(f32), scale_one,
+        w_qkv, latent_tokens, mid_grad, z_own, z_oth, o_own, o_oth, ada, shared.shape[0],
+    )
+    grad_qkv = jnp.transpose(grads[:3, :, :width], (1, 0, 2))
+    grad_proj = grads[3, :, :width].T
+    conditioning_grad = silu_pull(cond_row.reshape(1, width_full))[0]
+    fc1_rows = hidden // width
+    qkv_bias_grad = totals[6:8]
+    fc1_bias_grad = totals[8 : 8 + fc1_rows].reshape(hidden)
+    proj_bias_grad, fc2_bias_grad = totals[8 + fc1_rows :].reshape(2, width_full)
+    grad_ada_bias = totals[:6]
+    grad_ada = jnp.transpose(grad_ada, (1, 0, 2))
+    return (
+        layer_out,
+        tokens_grad,
+        conditioning_grad,
+        grad_qkv,
+        qkv_bias_grad,
+        grad_proj,
+        proj_bias_grad,
+        grad_fc1,
+        fc1_bias_grad,
+        grad_fc2,
+        fc2_bias_grad,
+        grad_ada,
+        grad_ada_bias,
+    )
+
+
 def solution(mesh):
     in_specs = (
         P(("dp", "tensor"), None),
@@ -285,4 +1158,5 @@
         P("dp", None, "tensor"),
         P(None, "tensor"),
     )
+    body = fast_body if fits(mesh) else general_body
     return jax.shard_map(body, mesh=mesh, in_specs=in_specs, out_specs=out_specs, check_vma=False)

time: 1490 us -> 502 us (0.34)
  waiting for transfers between devices: 1080 us -> 73.9 us
  Pallas kernels: 0 us -> 243 us
  matrix products: 220 us -> 33.7 us
  blocking collectives: 72.4 us -> 0 us
  starting transfers between devices: 0.79 us -> 41.8 us
  other arithmetic: 82.8 us -> 43.9 us
  local copies, waits for them, and re-layouts: 15.3 us -> 35.2 us
    reduce_scatter x8 -> x0, waiting for transfers between devices: 716 us -> none  [the longest x1 190 us: body(): lax.psum_scatter(grad_ada, 'dp', scatter_dimension=0, tiled=True)]
    all_gather x9 -> x2, waiting for transfers between devices: 365 us -> 33.3 us  [full_weight(): return lax.all_gather(shard, 'dp', axis=0, tiled=True)]
    pallas_call x0 -> x9, Pallas kernels: none -> 243 us  [the longest x1 131 us: close(): pl.pallas_call(functools.partial(close_kernel, n_dp=n_dp, n_mods=n_mods,...]
    dot_general x20 -> x9, matrix products: 220 us -> 33.7 us  [the longest x5 18.4 us: nn(): lax.dot_general(a, b, (((1,), (0,)), ((), ())), preferred_element_type=f32)]
    psum x2 -> x0, blocking collectives: 67.9 us -> none  [the longest x1 60.6 us: body(): lax.psum((qkv_bias_pair, tensor_totals[1], fc1_bias_part, tensor_totals[2...]
    ppermute x0 -> x34, starting transfers between devices: none -> 41.7 us  [the longest x15 23.5 us: shift(): lax.ppermute(values, 'dp', [(i, (i + 4 * step) % n_dp) for i in range(n_d...]
    ppermute x0 -> x34, waiting for transfers between devices: none -> 40.6 us  [the longest x9 26 us: swap(): return lax.ppermute(values, 'tensor', [(0, 1), (1, 0)])]
    reduce_sum x7 -> x2, other arithmetic: 31.7 us -> 3.5 us  [the longest x1 2.54 us: fast_body(): sums(out_grad * branch_two)]
  transfers between devices with their start and end apart: 19 -> 36, of which waited for: 16 -> 16; matrix products, arithmetic and copies ran while one was open for 9% -> 19% of each run, Pallas kernels for 0% -> 44%
where the time goes in v1:
time: 502 us; the launch traced here: 494 us
  Pallas kernels  243 us (48%)
  waiting for transfers between devices  73.9 us (15%)
  other arithmetic  43.9 us (9%)
  starting transfers between devices  41.8 us (8%)
  local copies, waits for them, and re-layouts  35.2 us (7%)
  matrix products  33.7 us (7%)
  between operations  22.5 us (4%)
    pallas_call x1, Pallas kernels, close(): pl.pallas_call(functools.partial(close_kernel, n_dp=n_dp, n_mods=n_mods,...  131 us
    pallas_call x1, Pallas kernels, attend_back(): pl.pallas_call(functools.partial(attend_back_kernel, heads=heads, block=m...  34.1 us
    all_gather x2, waiting for transfers between devices, full_weight(): return lax.all_gather(shard, 'dp', axis=0, tiled=True)  33.3 us
    pallas_call x2, Pallas kernels, feed(): pl.pallas_call(functools.partial(feed_kernel, steps=steps), grid=(steps,)...  29.8 us
    ppermute x9, waiting for transfers between devices, swap(): return lax.ppermute(values, 'tensor', [(0, 1), (1, 0)])  26 us
    ppermute x15, starting transfers between devices, shift(): lax.ppermute(values, 'dp', [(i, (i + 4 * step) % n_dp) for i in range(n_d...  23.5 us
    pallas_call x2, Pallas kernels, attend(): pl.pallas_call(functools.partial(attend_kernel, heads=heads, block=min(ro...  22 us
    pallas_call x2, Pallas kernels, outer(): pl.pallas_call(functools.partial(outer_kernel, lines=lines, block=block),...  21.9 us
  transfers between devices with their start and end apart: 36, of which 16 were waited for; matrix products, arithmetic and copies ran while one was open for 19% of the time, Pallas kernels for 44%

profile of v1, /device:TPU:0, one launch (start us, length us, event | category | flops | bytes accessed | tf_op | source)
XLA Modules:
  0.0 493.5 jit_solution(2159317224978038400)
XLA Ops:
  11.3 3.0 collective-permute-start
  14.3 2.6 collective-permute-start.1
  18.9 1.6 collective-permute-done.2
  20.6 1.6 collective-permute-start.3
  22.1 2.2 collective-permute-done.3
  30.0 1.6 collective-permute-start.6
  31.5 2.7 collective-permute-done.6
  34.5 3.7 collective-permute-start.8
  38.3 2.0 multiply_reduce_fusion.2
  42.0 1.6 collective-permute-start.10
  54.9 1.6 collective-permute-start.20
  62.5 2.0 collective-permute-done.13
  65.3 1.9 collective-permute-start.15
  71.3 2.1 all-gather.3.cloned.1.call-done
  73.4 5.6 %add_convert_fusion.1.own_ref.q_ref = bf16[512,1920]{1,0:T(8,128)(2,1)S(1)} fusion(bf16[512,1152]{1,0:T(8,128)(2,1)} %reduce-precision_convert_fusion.2.aown_ref, f32[1920]{0:T(1024)S(1)} %copy-done.50, bf16[1152,2560]{1,0:T(8,128)(2,1)} %all-gather.3.cloned.1.call-done), kind=kOutput, calls=%fused_computation.5 | convolution fusion | flops 2266890240 | bytes 7577088 | tf_op jit(solution)/shard_map/dot_general | solution.py:276
  80.4 4.1 add_convert_fusion.q_ref.oth_ref
  84.5 11.3 %shard_map.228 = (bf16[512,640]{1,0:T(8,128)(2,1)S(1)}, f32[8,512]{1,0:T(8,128)S(1)}) custom-call(bf16[512,1920]{1,0:T(8,128)(2,1)S(1)} %add_convert_fusion.q_ref.oth_ref, bf16[512,1920]{1,0:T(8,128)(2,1)S(1)} %add_convert_fusion.1.own_ref.q_ref, bf16[512,1920]{1,0:T(8,128)(2,1)S(1)} %add_convert_fusion.q_ref.oth_ref), custom_call_target="tpu_custom_call" | custom-call | flops 17179869184 | bytes 5242880 | tf_op jit(solution)/shard_map/pallas_call | solution.py:336
  97.9 10.8 %shard_map.229 = (bf16[512,640]{1,0:T(8,128)(2,1)S(1)}, f32[8,512]{1,0:T(8,128)S(1)}) custom-call(bf16[512,1920]{1,0:T(8,128)(2,1)S(1)} %add_convert_fusion.1.own_ref.q_ref, bf16[512,1920]{1,0:T(8,128)(2,1)S(1)} %add_convert_fusion.1.own_ref.q_ref, bf16[512,1920]{1,0:T(8,128)(2,1)S(1)} %add_convert_fusion.q_ref.oth_ref), custom_call_target="tpu_custom_call" | custom-call | flops 17179869184 | bytes 5242880 | tf_op jit(solution)/shard_map/pallas_call | solution.py:336
  108.7 18.0 %collective-permute-done.18 = f16[512,1152]{1,0:T(8,128)(2,1)S(1)} collective-permute-done((f16[512,1152]{1,0:T(8,128)(2,1)S(1)}, f16[512,1152]{1,0:T(8,128)(2,1)S(1)}, u32[]{:S(2)}, u32[]{:S(2)}) %collective-permute-start.18) | collective-permute-done | bytes 1179680 | tf_op jit(solution)/shard_map/ppermute | solution.py:905
  126.6 2.6 fusion.35
  132.4 31.2 %all-gather.5.cloned.1.call-done.w1_ref.w2_ref = bf16[1152,4608]{1,0:T(8,128)(2,1)} async-done(((bf16[72,4608]{1,0:T(8,128)(2,1)}), bf16[1152,4608]{1,0:T(8,128)(2,1)}) %all-gather.5.cloned.1.call-update) | async-done | bytes 10616848 | tf_op jit(solution)/shard_map/all_gather | solution.py:981
  164.3 14.5 %shard_map.230 = (bf16[512,2304]{1,0:T(8,128)(2,1)S(1)}, bf16[512,2304]{1,0:T(8,128)(2,1)}, f32[512,1152]{1,0:T(8,128)}) custom-call(bf16[512,1152]{1,0:T(8,128)(2,1)} %reduce-precision_convert_fusion.1.m_ref.lown_ref, bf16[512,1152]{1,0:T(8,128)(2,1)S(1)} %get-tuple-element.61.g_ref.lown_ref, bf16[1152,4608]{1,0:T(8,128)(2,1)} %all-gather.5.cloned.1.call-done.w1_ref.w2_ref, ...), custom_call_target="tpu_custom_call" | custom-call | flops 16307453952 | bytes 20054016 | tf_op jit(solution)/shard_map/pallas_call | solution.py:452
  178.8 15.3 %shard_map.231 = (bf16[512,2304]{1,0:T(8,128)(2,1)S(1)}, bf16[512,2304]{1,0:T(8,128)(2,1)}, bf16[512,1152]{1,0:T(8,128)(2,1)}) custom-call(bf16[512,1152]{1,0:T(8,128)(2,1)} %collective-permute-done.19.m_ref.loth_ref, bf16[512,1152]{1,0:T(8,128)(2,1)} %collective-permute-done.20.g_ref.loth_ref, ...), custom_call_target="tpu_custom_call" | custom-call | flops 16307453952 | bytes 20054016 | tf_op jit(solution)/shard_map/pallas_call | solution.py:452
  195.5 10.9 %shard_map.232 = (f32[2,4,72,2304]{3,2,1,0:T(8,128)}, f32[2,4,72,2304]{3,2,1,0:T(8,128)}, f32[8,2304]{1,0:T(8,128)}) custom-call(s32[1]{0:T(128)} %bitcast.21.core_ref, bf16[512,1152]{1,0:T(8,128)(2,1)S(1)} %get-tuple-element.61.g_ref.lown_ref, bf16[512,1152]{1,0:T(8,128)(2,1)} %collective-permute-done.20.g_ref.loth_ref, ...), custom_call_target="tpu_custom_call" | custom-call | flops 10871635968 | bytes 17694720 | tf_op jit(solution)/shard_map/pallas_call | solution.py:508
  206.7 11.0 %shard_map.233 = (f32[2,4,72,2304]{3,2,1,0:T(8,128)}, f32[2,4,72,2304]{3,2,1,0:T(8,128)}, f32[8,2304]{1,0:T(8,128)S(1)}) custom-call(s32[1]{0:T(128)} %bitcast.21.core_ref, bf16[512,1152]{1,0:T(8,128)(2,1)} %reduce-precision_convert_fusion.1.m_ref.lown_ref, bf16[512,1152]{1,0:T(8,128)(2,1)} %collective-permute-done.19.m_ref.loth_ref, ...), custom_call_target="tpu_custom_call" | custom-call | flops 10871635968 | bytes 17694720 | tf_op jit(solution)/shard_map/pallas_call | solution.py:508
  221.2 2.1 convert_bitcast_fusion.2.ada_any
  228.6 4.6 slice.94.w_any
  236.1 4.1 fusion.8
  240.7 6.2 %collective-permute-done.22.got_ref = bf16[512,1152]{1,0:T(8,128)(2,1)S(1)} collective-permute-done((bf16[512,1152]{1,0:T(8,128)(2,1)}, bf16[512,1152]{1,0:T(8,128)(2,1)S(1)}, u32[]{:S(2)}, u32[]{:S(2)}) %collective-permute-start.22) | collective-permute-done | bytes 1179680 | tf_op jit(solution)/shard_map/ppermute | solution.py:905
  246.9 1.7 copy-done.4
  248.6 3.8 shard_map.234
  252.4 1.5 collective-permute-start.24
  254.0 3.3 fusion.9
  257.3 6.9 %fusion.4 = bf16[512,1152]{1,0:T(8,128)(2,1)} fusion(bf16[512,2304]{1,0:T(8,128)(2,1)S(1)} %copy-done.16, bf16[1152,4608]{1,0:T(8,128)(2,1)} %all-gather.5.cloned.1.call-done.w1_ref.w2_ref), kind=kOutput, calls=%fused_computation.7 | convolution fusion | flops 2718498816 | bytes 8847360 | tf_op jit(solution)/shard_map/dot_general | solution.py:280
  264.3 4.7 fusion
  268.9 3.7 convolution_convert_fusion.1.gown_ref
  274.1 3.3 bitcast_add_fusion.1
  280.7 2.4 collective-permute-start.33
  283.7 3.7 convolution_convert_fusion.goth_ref
  288.7 34.1 %shard_map.235 = (bf16[512,1920]{1,0:T(8,128)(2,1)}, bf16[512,1920]{1,0:T(8,128)(2,1)}) custom-call(bf16[512,1920]{1,0:T(8,128)(2,1)} %copy-done.13, bf16[512,1920]{1,0:T(8,128)(2,1)} %copy-done.14, bf16[512,640]{1,0:T(8,128)(2,1)} %convolution_convert_fusion.1.gown_ref, bf16[512,640]{1,0:T(8,128)(2,1)} %convolution_convert_fusion.goth_ref, ...), custom_call_target="tpu_custom_call" | custom-call | flops 21474836480 | bytes 10485760 | tf_op jit(solution)/shard_map/pallas_call | solution.py:405
  322.9 2.4 fusion.18
  325.3 2.5 multiply_reduce_fusion
  330.9 3.3 bitcast_add_fusion
  336.6 2.9 collective-permute-start.30
  339.5 130.9 %shard_map.236 = (f32[512,1152]{1,0:T(8,128)}, f32[4,72,640]{2,1,0:T(8,128)}, f32[6,72,576]{2,1,0:T(8,128)}, f32[16,576]{1,0:T(8,128)}, f32[16,72]{1,0:T(8,128)}) custom-call(bf16[512,1152]{1,0:T(8,128)(2,1)} %reduce-precision_convert_fusion.2.aown_ref, bf16[512,1152]{1,0:T(8,128)(2,1)} %collective-permute-done.17.aoth_ref, ...), custom_call_target="tpu_custom_call" | custom-call | flops 60000002048 | bytes 100000000 | tf_op jit(solution)/shard_map/pallas_call | solution.py:824
  470.4 1.6 slice_bitcast_fusion.1
  478.9 2.0 slice_bitcast_fusion
  481.0 2.2 bitcast_add_fusion.3
  (257 shorter events, 71.6 us)
Async XLA Ops:
  7.2 66.2 %all-gather.3.cloned.1.call-start = ((), (), s32[]{:S(2)}) async-start(), calls=%async_computation | async-start | bytes 6266880 | tf_op jit(solution)/shard_map/all_gather | solution.py:981
  9.6 154.0 %all-gather.5.cloned.1.call-start = ((), (), s32[]{:S(2)}) async-start(), calls=%async_computation.1 | async-start | bytes 11280384 | tf_op jit(solution)/shard_map/all_gather | solution.py:981
  11.3 7.0 %collective-permute-start = (bf16[1,1152]{1,0:T(2,128)(2,1)S(1)}, bf16[1,1152]{1,0:T(2,128)(2,1)S(1)}, u32[]{:S(2)}, u32[]{:S(2)}) collective-permute-start(bf16[1,1152]{1,0:T(2,128)(2,1)S(1)} %get-tuple-element.120), channel_id=1, source_target_pairs={{0,8},{2,10},{4,12},{6,14},{8,16},{10,18},{12,20},{14,22},{16,24},... | collective-permute-start | bytes 6920 | tf_op jit(solution)/shard_map/ppermute | solution.py:911
  14.3 4.6 collective-permute-start.1
  16.9 3.6 collective-permute-start.2
  20.6 3.7 collective-permute-start.3
  24.3 1.9 collective-permute-start.4
  28.4 1.5 collective-permute-start.5
  30.0 4.2 collective-permute-start.6
  34.4 6.0 %collective-permute-start.7 = (f32[3456]{0:T(1024)S(1)}, f32[3456]{0:T(1024)S(1)}, u32[]{:S(2)}, u32[]{:S(2)}) collective-permute-start(f32[3456]{0:T(1024)S(1)} %get-tuple-element.99), channel_id=1, source_target_pairs={{0,8},{2,10},{4,12},{6,14},{8,16},{10,18},{12,20},{14,22},{16,24},... | collective-permute-start | bytes 41480 | tf_op jit(solution)/shard_map/ppermute | solution.py:911
  34.5 5.9 %collective-permute-start.8 = (f32[3456]{0:T(1024)S(1)}, f32[3456]{0:T(1024)S(1)}, u32[]{:S(2)}, u32[]{:S(2)}) collective-permute-start(f32[3456]{0:T(1024)S(1)} %get-tuple-element.101), channel_id=1, source_target_pairs={{0,16},{2,18},{4,20},{6,22},{8,24},{10,26},{12,28},{14,30},{16,0},... | collective-permute-start | bytes 41480 | tf_op jit(solution)/shard_map/ppermute | solution.py:911
  38.2 3.7 collective-permute-start.9
  42.0 3.8 collective-permute-start.10
  48.2 25.2 %copy-start.50 = (f32[1920]{0:T(1024)S(1)}, f32[1920]{0:T(1024)}, u32[]{:S(2)}) copy-start(f32[1920]{0:T(1024)} %add.352) | copy-start | bytes 23044
  48.2 9.6 %collective-permute-start.11 = (f32[1]{0:T(128)}, f32[1]{0:T(128)}, u32[]{:S(2)}, u32[]{:S(2)}) collective-permute-start(f32[1]{0:T(128)} %bitcast.16), channel_id=1, source_target_pairs={{0,1},{1,0},{2,3},{3,2},{4,5},{5,4},{6,7},{7,6},{8,9},{9,8},{10,11... | collective-permute-start | bytes 20 | tf_op jit(solution)/shard_map/ppermute | solution.py:905
  51.2 29.2 %collective-permute-start.17 = (bf16[512,1152]{1,0:T(8,128)(2,1)}, bf16[512,1152]{1,0:T(8,128)(2,1)}, u32[]{:S(2)}, u32[]{:S(2)}) collective-permute-start(bf16[512,1152]{1,0:T(8,128)(2,1)} %reduce-precision_convert_fusion.2.aown_ref), channel_id=1, source_target_pairs={{0,1},{1,0},{2,3},{3,2},{4,5},{5,4},{6,7},{7,6},{8,9},{9,8},{10,11... | collective-permute-start | bytes 3538952 | tf_op jit(solution)/shard_map/ppermute | solution.py:905
  54.9 77.5 %collective-permute-start.20 = (bf16[512,1152]{1,0:T(8,128)(2,1)S(1)}, bf16[512,1152]{1,0:T(8,128)(2,1)}, u32[]{:S(2)}, u32[]{:S(2)}) collective-permute-start(bf16[512,1152]{1,0:T(8,128)(2,1)S(1)} %get-tuple-element.61.g_ref.lown_ref), channel_id=1, source_target_pairs={{0,1},{1,0},{2,3},{3,2},{4,5},{5,4},{6,7},{7,6},{8,9},{9,8},{10,11... | collective-permute-start | bytes 3538952 | tf_op jit(solution)/shard_map/ppermute | solution.py:905
  59.8 1.1 collective-permute-start.12
  61.0 3.5 collective-permute-start.13
  64.6 5.3 %collective-permute-start.14 = (f32[2]{0:T(128)S(1)}, f32[2]{0:T(128)S(1)}, u32[]{:S(2)}, u32[]{:S(2)}) collective-permute-start(f32[2]{0:T(128)S(1)} %fusion.49), channel_id=1, source_target_pairs={{0,8},{2,10},{4,12},{6,14},{8,16},{10,18},{12,20},{14,22},{16,24},... | collective-permute-start | bytes 32 | tf_op jit(solution)/shard_map/ppermute | solution.py:911
  65.3 4.7 collective-permute-start.15
  67.1 3.5 collective-permute-start.16
  97.0 29.6 %copy-start.22 = (f32[512,1152]{1,0:T(8,128)S(1)}, f32[512,1152]{1,0:T(8,128)}, u32[]{:S(2)}) copy-start(f32[512,1152]{1,0:T(8,128)} %x_any.1) | copy-start | bytes 7077892
  97.1 29.6 %copy-start.39 = (f32[1152]{0:T(1024)S(1)}, f32[1152]{0:T(1024)}, u32[]{:S(2)}) copy-start(f32[1152]{0:T(1024)} %get-tuple-element.116) | copy-start | bytes 13828
  97.1 29.6 %copy-start.51 = (f32[1152]{0:T(1024)S(1)}, f32[1152]{0:T(1024)}, u32[]{:S(2)}) copy-start(f32[1152]{0:T(1024)} %param.19) | copy-start | bytes 13828
  97.1 29.5 %collective-permute-start.18 = (f16[512,1152]{1,0:T(8,128)(2,1)S(1)}, f16[512,1152]{1,0:T(8,128)(2,1)S(1)}, u32[]{:S(2)}, u32[]{:S(2)}) collective-permute-start(f16[512,1152]{1,0:T(8,128)(2,1)S(1)} %fusion.7), channel_id=1, source_target_pairs={{0,1},{1,0},{2,3},{3,2},{4,5},{5,4},{6,7},{7,6},{8,9},{9,8},{10,11... | collective-permute-start | bytes 3538952 | tf_op jit(solution)/shard_map/ppermute | solution.py:905
  108.6 20.6 %copy-start.5 = (bf16[512,640]{1,0:T(8,128)(2,1)}, bf16[512,640]{1,0:T(8,128)(2,1)S(1)}, u32[]{:S(2)}) copy-start(bf16[512,640]{1,0:T(8,128)(2,1)S(1)} %get-tuple-element.59.oown_any) | copy-start | bytes 1966084
  108.7 20.6 %copy-start.19 = (f32[8,512]{1,0:T(8,128)}, f32[8,512]{1,0:T(8,128)S(1)}, u32[]{:S(2)}) copy-start(f32[8,512]{1,0:T(8,128)S(1)} %get-tuple-element.84.lown_ref) | copy-start | bytes 49156
  131.4 47.4 %collective-permute-start.19 = (bf16[512,1152]{1,0:T(8,128)(2,1)}, bf16[512,1152]{1,0:T(8,128)(2,1)}, u32[]{:S(2)}, u32[]{:S(2)}) collective-permute-start(bf16[512,1152]{1,0:T(8,128)(2,1)} %reduce-precision_convert_fusion.1.m_ref.lown_ref), channel_id=1, source_target_pairs={{0,1},{1,0},{2,3},{3,2},{4,5},{5,4},{6,7},{7,6},{8,9},{9,8},{10,11... | collective-permute-start | bytes 3538952 | tf_op jit(solution)/shard_map/ppermute | solution.py:905
  206.5 29.6 %collective-permute-start.23 = (f32[2,4,72,2304]{3,2,1,0:T(8,128)}, f32[2,4,72,2304]{3,2,1,0:T(8,128)}, u32[]{:S(2)}, u32[]{:S(2)}) collective-permute-start(f32[2,4,72,2304]{3,2,1,0:T(8,128)} %get-tuple-element.67), channel_id=1, source_target_pairs={{0,2},{2,0},{4,6},{6,4},{8,10},{10,8},{12,14},{14,12},{16,18},{18,... | collective-permute-start | bytes 15925256 | tf_op jit(solution)/shard_map/ppermute | solution.py:908
  218.3 35.7 %collective-permute-start.21 = (f32[2,4,72,2304]{3,2,1,0:T(8,128)}, f32[2,4,72,2304]{3,2,1,0:T(8,128)}, u32[]{:S(2)}, u32[]{:S(2)}) collective-permute-start(f32[2,4,72,2304]{3,2,1,0:T(8,128)} %get-tuple-element.71), channel_id=1, source_target_pairs={{0,2},{2,0},{4,6},{6,4},{8,10},{10,8},{12,14},{14,12},{16,18},{18,... | collective-permute-start | bytes 15925256 | tf_op jit(solution)/shard_map/ppermute | solution.py:908
  218.6 28.3 %collective-permute-start.22 = (bf16[512,1152]{1,0:T(8,128)(2,1)}, bf16[512,1152]{1,0:T(8,128)(2,1)S(1)}, u32[]{:S(2)}, u32[]{:S(2)}) collective-permute-start(bf16[512,1152]{1,0:T(8,128)(2,1)} %get-tuple-element.65), channel_id=1, source_target_pairs={{0,1},{1,0},{2,3},{3,2},{4,5},{5,4},{6,7},{7,6},{8,9},{9,8},{10,11... | collective-permute-start | bytes 3538952 | tf_op jit(solution)/shard_map/ppermute | solution.py:905
  240.1 34.0 %collective-permute-start.25 = (f16[4,72,2304]{2,1,0:T(8,128)(2,1)}, f16[4,72,2304]{2,1,0:T(8,128)(2,1)}, u32[]{:S(2)}, u32[]{:S(2)}) collective-permute-start(f16[4,72,2304]{2,1,0:T(8,128)(2,1)} %fusion.8), channel_id=1, source_target_pairs={{0,4},{2,6},{4,0},{6,2},{8,12},{10,14},{12,8},{14,10},{16,20},{18,... | collective-permute-start | bytes 3981320 | tf_op jit(solution)/shard_map/ppermute | solution.py:908
  252.4 31.2 %collective-permute-start.24 = (bf16[512,1152]{1,0:T(8,128)(2,1)}, bf16[512,1152]{1,0:T(8,128)(2,1)}, u32[]{:S(2)}, u32[]{:S(2)}) collective-permute-start(bf16[512,1152]{1,0:T(8,128)(2,1)} %get-tuple-element.80.zown_any), channel_id=1, source_target_pairs={{0,1},{1,0},{2,3},{3,2},{4,5},{5,4},{6,7},{7,6},{8,9},{9,8},{10,11... | collective-permute-start | bytes 3538952 | tf_op jit(solution)/shard_map/ppermute | solution.py:905
  278.7 44.2 %collective-permute-start.31 = (f16[72,2304]{1,0:T(8,128)(2,1)}, f16[72,2304]{1,0:T(8,128)(2,1)}, u32[]{:S(2)}, u32[]{:S(2)}) collective-permute-start(f16[72,2304]{1,0:T(8,128)(2,1)} %get-tuple-element.129), channel_id=1, source_target_pairs={{0,8},{2,10},{4,12},{6,14},{8,16},{10,18},{12,20},{14,22},{16,24},... | collective-permute-start | bytes 995336 | tf_op jit(solution)/shard_map/ppermute | solution.py:911
  279.1 43.7 %collective-permute-start.32 = (f16[72,2304]{1,0:T(8,128)(2,1)}, f16[72,2304]{1,0:T(8,128)(2,1)}, u32[]{:S(2)}, u32[]{:S(2)}) collective-permute-start(f16[72,2304]{1,0:T(8,128)(2,1)} %get-tuple-element.128), channel_id=1, source_target_pairs={{0,16},{2,18},{4,20},{6,22},{8,24},{10,26},{12,28},{14,30},{16,0},... | collective-permute-start | bytes 995336 | tf_op jit(solution)/shard_map/ppermute | solution.py:911
  280.7 42.2 %collective-permute-start.33 = (f16[72,2304]{1,0:T(8,128)(2,1)}, f16[72,2304]{1,0:T(8,128)(2,1)}, u32[]{:S(2)}, u32[]{:S(2)}) collective-permute-start(f16[72,2304]{1,0:T(8,128)(2,1)} %get-tuple-element.127), channel_id=1, source_target_pairs={{0,24},{2,26},{4,28},{6,30},{8,0},{10,2},{12,4},{14,6},{16,8},{18,... | collective-permute-start | bytes 995336 | tf_op jit(solution)/shard_map/ppermute | solution.py:911
  283.1 47.8 %collective-permute-start.27 = (f16[4,72,2304]{2,1,0:T(8,128)(2,1)}, f16[4,72,2304]{2,1,0:T(8,128)(2,1)}, u32[]{:S(2)}, u32[]{:S(2)}) collective-permute-start(f16[4,72,2304]{2,1,0:T(8,128)(2,1)} %fusion.9), channel_id=1, source_target_pairs={{0,4},{2,6},{4,0},{6,2},{8,12},{10,14},{12,8},{14,10},{16,20},{18,... | collective-permute-start | bytes 3981320 | tf_op jit(solution)/shard_map/ppermute | solution.py:908
  287.4 37.9 %collective-permute-start.26 = (bf16[512,1152]{1,0:T(8,128)(2,1)}, bf16[512,1152]{1,0:T(8,128)(2,1)S(1)}, u32[]{:S(2)}, u32[]{:S(2)}) collective-permute-start(bf16[512,1152]{1,0:T(8,128)(2,1)} %fusion.4), channel_id=1, source_target_pairs={{0,1},{1,0},{2,3},{3,2},{4,5},{5,4},{6,7},{7,6},{8,9},{9,8},{10,11... | collective-permute-start | bytes 3538952 | tf_op jit(solution)/shard_map/ppermute | solution.py:905
  288.7 36.6 %copy-start.2 = (f32[512,1152]{1,0:T(8,128)S(1)}, f32[512,1152]{1,0:T(8,128)}, u32[]{:S(2)}) copy-start(f32[512,1152]{1,0:T(8,128)} %grad_ref.1) | copy-start | bytes 7077892
  288.7 36.6 %copy-start.28 = (f32[512,1152]{1,0:T(8,128)S(1)}, f32[512,1152]{1,0:T(8,128)}, u32[]{:S(2)}) copy-start(f32[512,1152]{1,0:T(8,128)} %fusion) | copy-start | bytes 7077892
  288.7 36.6 %copy-start.34 = (f32[1152]{0:T(1024)S(1)}, f32[1152]{0:T(1024)}, u32[]{:S(2)}) copy-start(f32[1152]{0:T(1024)} %copy-done.33) | copy-start | bytes 13828
  288.7 36.6 %copy-start.48 = (f32[1152]{0:T(1024)S(1)}, f32[1152]{0:T(1024)}, u32[]{:S(2)}) copy-start(f32[1152]{0:T(1024)} %param.23) | copy-start | bytes 13828
  335.1 145.8 %collective-permute-start.28 = (f16[72,2304]{1,0:T(8,128)(2,1)}, f16[72,2304]{1,0:T(8,128)(2,1)}, u32[]{:S(2)}, u32[]{:S(2)}) collective-permute-start(f16[72,2304]{1,0:T(8,128)(2,1)} %get-tuple-element.126), channel_id=1, source_target_pairs={{0,8},{2,10},{4,12},{6,14},{8,16},{10,18},{12,20},{14,22},{16,24},... | collective-permute-start | bytes 995336 | tf_op jit(solution)/shard_map/ppermute | solution.py:911
  335.1 145.8 %collective-permute-start.29 = (f16[72,2304]{1,0:T(8,128)(2,1)S(1)}, f16[72,2304]{1,0:T(8,128)(2,1)}, u32[]{:S(2)}, u32[]{:S(2)}) collective-permute-start(f16[72,2304]{1,0:T(8,128)(2,1)S(1)} %get-tuple-element.125), channel_id=1, source_target_pairs={{0,16},{2,18},{4,20},{6,22},{8,24},{10,26},{12,28},{14,30},{16,0},... | collective-permute-start | bytes 995336 | tf_op jit(solution)/shard_map/ppermute | solution.py:911
  336.6 144.4 %collective-permute-start.30 = (f16[72,2304]{1,0:T(8,128)(2,1)S(1)}, f16[72,2304]{1,0:T(8,128)(2,1)}, u32[]{:S(2)}, u32[]{:S(2)}) collective-permute-start(f16[72,2304]{1,0:T(8,128)(2,1)S(1)} %get-tuple-element.124), channel_id=1, source_target_pairs={{0,24},{2,26},{4,28},{6,30},{8,0},{10,2},{12,4},{14,6},{16,8},{18,... | collective-permute-start | bytes 995336 | tf_op jit(solution)/shard_map/ppermute | solution.py:911
  339.5 133.3 %copy-start.44 = (f32[1,1152]{1,0:T(1,128)S(1)}, f32[1,1152]{1,0:T(1,128)}, u32[]{:S(2)}) copy-start(f32[1,1152]{1,0:T(1,128)} %param.14) | copy-start | bytes 13828
  339.5 133.3 %copy-start.45 = (f32[1,1152]{1,0:T(1,128)S(1)}, f32[1,1152]{1,0:T(1,128)}, u32[]{:S(2)}) copy-start(f32[1,1152]{1,0:T(1,128)} %get-tuple-element.121) | copy-start | bytes 13828
  (44 other events, 303.0 us)
Sparse Core Ops, SparseCore 0:
  10.9 62.4 all-gather.2
  76.2 87.2 all-gather.4
